TPU v7x, 256 devices: a whole 4x4x8 slice. The times are simulated.
256 devices in a mesh: fn: 64 (over z, x, core), sub: 4 (over y).
Axes of the slice: x: 4, y: 4, z: 8, core: 2. Of those that a mesh axis runs over, the one named last changes fastest.
Arguments:
- coeffs: float32 [8192, 4, 16, 128], P('fn', None, 'sub'), may hold values from -6 to 6
- offsets: int32 [8192], replicated, may hold values from 0 to 1023, as said below
- potential: float32 [1024, 16, 128], P(None, 'sub'), may hold values from -1.5 to 1.5
Outputs:
- gradient: float32 [8192, 4, 16, 128], P('fn', None, 'sub')
Inputs may be any that keep to these rules, and one draw needn't show every extreme that they name: `offsets`: Nondecreasing; each grid plane is the first plane of 1 to 15 boxes, both ends reached, on average 8; at most 46 boxes cover any plane (boxes wrap around the periodic wire), and some plane is covered by exactly 46.
All inputs are finite; a program needn't handle non-finite values.
Results may differ from a plain program's by a relative error of at most 0.0003.
Values sent between devices are 32-bit elements; how exact they have to be, the bound alone decides.
No kernel may reach another device: no remote copies, remote signals or barrier semaphores. Data moves between devices by JAX's collectives and lax.ppermute only.
A program may use at most 64 MiB of HBM per device.

v0:
```python
import jax
import jax.numpy as jnp
from jax import lax
from jax.sharding import Mesh
from jax.sharding import PartitionSpec as P

PB = 4
CY = 16
CZ = 128
SWING = 7
KMAX = 46
FN = ("fn_0", "fn_1", "fn_2")


penalty = 0.5
highest = lax.Precision.HIGHEST


def extended(cells, sides, width, closed):
    for axis, dim in sides:
        count = lax.axis_size(axis)
        ends = count if closed else count - 1
        head = lax.slice_in_dim(cells, 0, width, axis=dim)
        tail = lax.slice_in_dim(cells, cells.shape[dim] - width, cells.shape[dim], axis=dim)
        cells = jnp.concatenate(
            [
                lax.ppermute(tail, axis, [(i, (i + 1) % count) for i in range(ends)]),
                cells,
                lax.ppermute(head, axis, [((i + 1) % count, i) for i in range(ends)]),
            ],
            axis=dim,
        )
    return cells


def copy_for_each(array, axis):
    copies = jnp.broadcast_to(array, (lax.axis_size(axis), *array.shape))
    return lax.all_to_all(copies, axis, split_axis=0, concat_axis=0, tiled=True)


def over_copies(array, axis):
    return copy_for_each(array, axis).sum(axis=0)


def cut_along(array, dim, size):
    lengths = array.shape
    tiles = array.reshape(*lengths[:dim], size, lengths[dim] // size, *lengths[dim + 1 :])
    return jnp.moveaxis(tiles, dim, 0)


def in_order(tiles, dim):
    lengths = list(tiles.shape[1:])
    lengths[dim] *= tiles.shape[0]
    return jnp.moveaxis(tiles, 0, dim).reshape(lengths)


def exchange_in_order(tiles, axes, order):
    lengths = [lax.axis_size(a) for a in axes]
    tiles = tiles.reshape(*lengths, *tiles.shape[1:])
    for k in order:
        tiles = lax.all_to_all(tiles, axes[k], split_axis=k, concat_axis=k, tiled=True)
    return tiles.reshape(-1, *tiles.shape[len(axes) :])


def exchange_by_chip(array, groups, order, split_dim, concat_dim):
    size = lax.axis_size(groups[0]) * lax.axis_size(groups[1])
    tiles = cut_along(array, split_dim, size)
    return in_order(exchange_in_order(tiles, groups, order), concat_dim)


def kinetic(box_data, padded_y):
    padded_x = jnp.pad(box_data, ((0, 0), (1, 1), (0, 0), (0, 0)))
    padded_z = jnp.pad(box_data, ((0, 0), (0, 0), (0, 0), (1, 1)))
    beside = padded_x[:, 2:] + padded_x[:, :-2]
    beside = beside + padded_y[:, :, 2:] + padded_y[:, :, :-2]
    beside = beside + padded_z[..., 2:] + padded_z[..., :-2]
    return -0.5 * (beside - 6.0 * box_data)


def to_band(gram_block):
    width = gram_block.shape[0]
    row_ids = jnp.arange(width, dtype=jnp.int32)[:, None]
    col_ids = row_ids + jnp.arange(128, dtype=jnp.int32)[None, :] - 64
    inside = (col_ids >= 0) & (col_ids < width)
    picked = jnp.take_along_axis(gram_block, jnp.clip(col_ids, 0, width - 1), axis=1)
    return jnp.where(inside, picked, 0.0)


def from_band(band_rows):
    width = band_rows.shape[0]
    index_map = (
        jnp.arange(width, dtype=jnp.int32)[None, :]
        - jnp.arange(width, dtype=jnp.int32)[:, None]
        + 64
    )
    return jnp.take_along_axis(band_rows, index_map, axis=1)


def selector(index, count):
    return (index[None, :] == jnp.arange(count, dtype=jnp.int32)[:, None]).astype(jnp.float32)


def select_rows(matrix, data):
    return jnp.dot(matrix, data, precision=highest)


def select_back(matrix, data):
    return lax.dot_general(matrix, data, (((0,), (0,)), ((), ())), precision=highest)


def body(coeffs, offsets, potential):
    peer_count = lax.axis_size(FN)
    position = lax.axis_index(FN)
    local_funcs, box_len, rows_y, depth_cells = coeffs.shape
    total_funcs = offsets.shape[0]
    planes = potential.shape[0]
    slab_planes = planes // peer_count
    cell_count = rows_y * depth_cells
    per_plane = total_funcs // planes
    reach = per_plane * (slab_planes + box_len - 1) + 2 * SWING
    capacity = box_len * ((reach + peer_count - 1) // peer_count)
    slot_total = peer_count * capacity
    volume = 1.0 / (PB * CY * CZ)
    piece_range = jnp.arange(box_len, dtype=jnp.int32)
    peer_range = jnp.arange(peer_count, dtype=jnp.int32)
    bounds = jnp.searchsorted(offsets, jnp.arange(planes + 1, dtype=jnp.int32), side="left")
    counts = bounds[1:] - bounds[:-1]
    firsts = bounds[:-1]
    func_ids = jnp.arange(local_funcs, dtype=jnp.int32) * peer_count + position
    box_planes = (offsets[func_ids][:, None] + piece_range[None, :]) % planes
    owners = (box_planes // slab_planes).reshape(-1)
    onehot = (owners[:, None] == peer_range[None, :]).astype(jnp.int32)
    ranks = jnp.sum((jnp.cumsum(onehot, axis=0) - onehot) * onehot, axis=1)
    send_slot = owners * capacity + ranks
    send_map = selector(send_slot, slot_total)
    padded_y = extended(coeffs, (("sub", 2),), 1, False)
    plane_map = (
        box_planes.reshape(-1)[:, None] == jnp.arange(planes, dtype=jnp.int32)[None, :]
    ).astype(jnp.float32)
    local_potential = select_rows(plane_map, potential.reshape(planes, cell_count)).reshape(
        local_funcs, box_len, rows_y, depth_cells
    )
    applied = kinetic(coeffs, padded_y) + local_potential * coeffs
    outgoing = jnp.stack([coeffs, applied], axis=2).reshape(local_funcs * box_len, 2 * cell_count)
    send_buffer = select_rows(send_map, outgoing)
    arrived = lax.all_to_all(
        send_buffer.reshape(peer_count, capacity, 2, cell_count),
        FN,
        split_axis=0,
        concat_axis=0,
        tiled=True,
    )
    channels = 2
    source_ids = (
        jnp.arange(local_funcs, dtype=jnp.int32)[None, :] * peer_count + peer_range[:, None]
    )
    source_planes = (offsets[source_ids][..., None] + piece_range) % planes
    source_funcs = jnp.broadcast_to(source_ids[..., None], source_planes.shape).reshape(
        peer_count, -1
    )
    source_planes = source_planes.reshape(peer_count, -1)
    mine = (source_planes // slab_planes == position).astype(jnp.int32)
    ranks_in = jnp.cumsum(mine, axis=1) - mine
    slot_flat = jnp.where(mine > 0, peer_range[:, None] * capacity + ranks_in, slot_total).reshape(
        -1
    )
    slot_func = (
        jnp.full((slot_total,), -1, jnp.int32)
        .at[slot_flat]
        .set(source_funcs.reshape(-1), mode="drop")
    )
    slot_plane = (
        jnp.zeros((slot_total,), jnp.int32)
        .at[slot_flat]
        .set(source_planes.reshape(-1), mode="drop")
    )
    slot_live = slot_func >= 0
    my_planes = position * slab_planes + jnp.arange(slab_planes, dtype=jnp.int32)
    plane_first = firsts[(my_planes - (box_len - 1)) % planes]
    plane_count = jnp.zeros((slab_planes,), jnp.int32)
    for back_step in range(box_len):
        plane_count = plane_count + counts[(my_planes - back_step) % planes]
    local_plane = jnp.clip(slot_plane - position * slab_planes, 0, slab_planes - 1)
    slot_in_plane = (slot_func - plane_first[local_plane]) % total_funcs
    grid_index = jnp.where(slot_live, local_plane * KMAX + slot_in_plane, slab_planes * KMAX)
    grid_map = selector(grid_index, slab_planes * KMAX)
    grid = select_rows(grid_map, arrived.reshape(slot_total, channels * cell_count)).reshape(
        slab_planes, KMAX, channels, cell_count
    )
    values = grid[:, :, 0]
    slot_range = jnp.arange(KMAX, dtype=jnp.int32)
    is_live = slot_range[None, :] < plane_count[:, None]
    members = (plane_first[:, None] + slot_range[None, :]) % total_funcs
    images = grid[:, :, 1]
    gram_blocks = volume * jnp.einsum(
        "qac,qbc->qab", values, images - penalty * values, precision=highest
    )
    band_blocks = jax.vmap(to_band)(gram_blocks)
    own_start = firsts[(position * slab_planes - (box_len - 1)) % planes]
    prev_start = firsts[((position - 1) % peer_count * slab_planes - (box_len - 1)) % planes]
    next_start = firsts[((position + 1) % peer_count * slab_planes - (box_len - 1)) % planes]
    window_index = (members - own_start) % total_funcs
    targets = jnp.where(is_live, window_index, reach)
    partial_window = (
        jnp.zeros((reach, 128), jnp.float32)
        .at[targets.reshape(-1)]
        .add(band_blocks.reshape(-1, 128), mode="drop")
    )
    rows_here = jnp.arange(reach, dtype=jnp.int32)
    from_prev = (own_start + rows_here - prev_start) % total_funcs
    from_next = (own_start + rows_here - next_start) % total_funcs
    stacked = extended(partial_window[None], ((FN, 0),), 1, True)
    merged = stacked[1]
    merged = merged + stacked[0][jnp.clip(from_prev, 0, reach - 1)] * (from_prev < reach)[:, None]
    merged = merged + stacked[2][jnp.clip(from_next, 0, reach - 1)] * (from_next < reach)[:, None]
    merged = over_copies(merged, "sub")
    member_rows = merged[jnp.clip(window_index, 0, reach - 1)]
    mixing = jax.vmap(from_band)(member_rows) * is_live[:, None, :]
    updates = (
        images - jnp.einsum("qac,qcx->qax", mixing, values, precision=highest) - penalty * values
    )
    returning = select_back(grid_map, updates.reshape(slab_planes * KMAX, cell_count)).reshape(
        peer_count, capacity, cell_count
    )
    returned = exchange_by_chip(returning, (("fn_0", "fn_1"), "fn_2"), (1, 0), 0, 0)
    gradient = select_back(send_map, returned.reshape(slot_total, cell_count))
    return gradient.reshape(local_funcs, box_len, rows_y, depth_cells)


def solution(mesh):
    finer = Mesh(mesh.devices.reshape(8, 4, 2, mesh.shape["sub"]), ("fn_0", "fn_1", "fn_2", "sub"))
    return jax.shard_map(
        body,
        mesh=finer,
        in_specs=(P(FN, None, "sub", None), P(), P(None, "sub", None)),
        out_specs=P(FN, None, "sub", None),
        check_vma=False,
    )
```

profile of v0, /device:TPU:1, one launch (start us, length us, event | category | flops | bytes accessed | tf_op | source)
XLA Modules:
  0.0 666.5 jit_solution(5406049854195930328)
XLA Ops:
  3.7 5.4 collective-permute-start.1
  9.1 87.8 %while.24 = (s32[]{:T(128)}, u32[1025]{0:T(1024)S(1)}, u32[1025]{0:T(1024)S(1)}, s32[8192]{0:T(1024)S(1)}, s32[]{:T(128)}, /*index=5*/s32[]{:T(128)}, s32[]{}) while((s32[]{:T(128)}, u32[1025]{0:T(1024)S(1)}, u32[1025]{0:T(1024)S(1)}, s32[8192]{0:T(1024)S(1)}, s32[]{:T(128)}, /*index=5*/s32[]{:T(128)}, s32[]{}) %tuple.64), condition=%wide.region_8.9_spmd.clone, body=%wide.region_7.8_spmd.clone.sunk | while | flops 20502 | bytes 75943 | solution.py:126
  9.1 6.2 gather_fusion
  15.4 6.2 gather_fusion
  21.7 6.2 gather_fusion
  27.9 6.2 gather_fusion
  34.2 6.2 gather_fusion
  40.5 6.2 gather_fusion
  46.7 6.2 gather_fusion
  53.0 6.2 gather_fusion
  59.3 6.2 gather_fusion
  65.6 6.2 gather_fusion
  71.8 6.2 gather_fusion
  78.1 6.2 gather_fusion
  84.4 6.2 gather_fusion
  90.6 6.2 gather_fusion
  96.9 45.5 %gather_fusion.2 = s32[8192]{0:T(1024)S(1)} fusion(s32[8192]{0:T(1024)S(1)} %get-tuple-element.187, s32[8192]{0:T(1024)S(1)} %fusion.79), kind=kCustom, calls=%fused_computation.2 | custom fusion | bytes 98304 | tf_op jit(solution)/shard_map/gather | solution.py:157
  152.2 6.1 add.846
  181.3 13.4 %all-to-all-start = ((f32[64,12,2,512]{3,2,1,0:T(2,128)}), f32[64,12,2,512]{3,2,1,0:T(2,128)S(1)}, u32[]{:S(2)}, u32[]{:S(2)}) async-start(f32[64,12,2,512]{3,2,1,0:T(2,128)} %copy.192), calls=%async_computation | async-start | bytes 6291456 | tf_op jit(solution)/shard_map/all_to_all | solution.py:146
  201.6 4.9 add.864
  209.5 4.9 reshape.1292
  214.4 120.3 %scatter_custom_fusion.1 = s32[768]{0:T(1024)S(1)} fusion(s32[32768]{0:T(1024)} %bitcast.211, s32[32768]{0:T(1024)S(1)} %add_select_fusion, s32[]{:T(128)} %constant.276.clone.1), kind=kCustom, calls=%fused_computation.256 | custom fusion | bytes 3584 | tf_op jit(solution)/shard_map/scatter | solution.py:175
  334.7 120.3 %scatter_custom_fusion = s32[768]{0:T(1024)S(1)} fusion(s32[32768]{0:T(1024)} %bitcast.212, s32[32768]{0:T(1024)S(1)} %reshape.1292, s32[]{:T(128)} %constant.283.clone.1), kind=kCustom, calls=%fused_computation.258 | custom fusion | bytes 3584 | tf_op jit(solution)/shard_map/scatter | solution.py:170
  463.5 10.0 %fusion.105 = s32[768]{0:T(1024)S(1)} fusion(s32[768]{0:T(1024)S(1)} %scatter_custom_fusion, s32[768]{0:T(1024)S(1)} %scatter_custom_fusion.1, s32[]{:T(128)} %bitcast.11, s32[]{:T(128)} %bitcast.12, s32[]{:T(128)} %bitcast.13, s32[]{:T(128)} %bitcast.14, s32[]{:T(128)} %bitcast.15, s32[]{:T(128)} %bitcast.16, s32[]{:T(128)} %bitcast.17, s32[]{:T(128)} %bitcast.18, ...), kind=kLoop, calls=%fused_computation.201 | loop fusion | flops 39168 | bytes 9284 | tf_op jit(solution)/shard_map/jit(_where)/select_n | solution.py:185
  486.4 50.1 %gather_fusion.11 = f32[5888,16]{1,0:T(8,128)} fusion(f32[16,46,46]{0,2,1:T(8,128)S(1)} %copy.195, s32[5888]{0:T(1024)S(1)} %fusion.83), kind=kCustom, calls=%fused_computation.11 | custom fusion | bytes 800768 | tf_op jit(solution)/shard_map/vmap(jit(take_along_axis))/gather | solution.py:85
  538.9 6.1 scatter_custom_fusion.2
  552.7 4.2 all-to-all-start.1
  557.3 5.5 all-to-all-done.1
  566.1 27.2 %gather_fusion.12 = f32[2116,16]{1,0:T(8,128)} fusion(f32[16,46,128]{0,2,1:T(8,128)S(1)} %copy.198, s32[2116]{0:T(1024)S(1)} %reshape.1282), kind=kCustom, calls=%fused_computation.12 | custom fusion | bytes 287776 | tf_op jit(solution)/shard_map/vmap(jit(take_along_axis))/gather | solution.py:96
  601.3 8.3 %all_to_all.20 = f32[32,2,1,12,512]{4,0,3,2,1:T(8,128)S(1)} all-to-all(f32[32,2,1,12,512]{4,0,3,2,1:T(8,128)S(1)} %fusion.20), channel_id=1, replica_groups=mesh['fn_0'=8,'fn_1'=4,'fn_2'=2,'sub'=4] {'fn_2'}, dimensions={1} | all-to-all | bytes 3145728 | tf_op jit(solution)/shard_map/all_to_all | solution.py:61
  612.0 8.0 %all-to-all-start.3 = ((f32[32,2,1,12,512]{4,1,3,2,0:T(2,128)}), f32[32,2,1,12,512]{4,1,3,2,0:T(2,128)}, u32[]{:S(2)}, u32[]{:S(2)}) async-start(f32[32,2,1,12,512]{4,1,3,2,0:T(2,128)} %copy.201), calls=%async_computation.3 | async-start | bytes 3145728 | tf_op jit(solution)/shard_map/all_to_all | solution.py:61
  620.1 37.7 %all-to-all-done.3 = f32[32,2,1,12,512]{4,1,3,2,0:T(2,128)} async-done(((f32[32,2,1,12,512]{4,1,3,2,0:T(2,128)}), f32[32,2,1,12,512]{4,1,3,2,0:T(2,128)}, u32[]{:S(2)}, u32[]{:S(2)}) %all-to-all-start.3) | async-done | bytes 1572896 | tf_op jit(solution)/shard_map/all_to_all | solution.py:61
  (221 shorter events, 100.3 us)
Async XLA Ops:
  0.0 9.1 %copy-start = (s32[8192]{0:T(1024)S(1)}, s32[8192]{0:T(1024)}, u32[]{:S(2)}) copy-start(s32[8192]{0:T(1024)} %param.6) | copy-start | bytes 98308
  2.4 162.4 %collective-permute-start = (f32[128,4,1,128]{3,0,2,1:T(8,128)}, f32[128,4,1,128]{3,0,2,1:T(8,128)}, u32[]{:S(2)}, u32[]{:S(2)}) collective-permute-start(f32[128,4,1,128]{3,0,2,1:T(8,128)} %get-tuple-element.100), channel_id=1, source_target_pairs={{1,0},{2,1},{3,2},{5,4},{6,5},{7,6},{9,8},{10,9},{11,10},{13,12},{... | collective-permute-start | bytes 786440 | tf_op jit(solution)/shard_map/ppermute | solution.py:29
  3.7 161.1 %collective-permute-start.1 = (f32[128,4,1,128]{3,0,2,1:T(8,128)}, f32[128,4,1,128]{3,0,2,1:T(8,128)}, u32[]{:S(2)}, u32[]{:S(2)}) collective-permute-start(f32[128,4,1,128]{3,0,2,1:T(8,128)} %get-tuple-element.101), channel_id=1, source_target_pairs={{0,1},{1,2},{2,3},{4,5},{5,6},{6,7},{8,9},{9,10},{10,11},{12,13},{... | collective-permute-start | bytes 786440 | tf_op jit(solution)/shard_map/ppermute | solution.py:27
  9.1 87.8 %copy-start.7 = (s32[128]{0:T(128)}, s32[128]{0:T(128)S(1)}, u32[]{:S(2)}) copy-start(s32[128]{0:T(128)S(1)} %iota_multiply_fusion.1) | copy-start | bytes 1540
  142.4 6.7 %copy-start.2 = (s32[8192]{0:T(1024)}, s32[8192]{0:T(1024)S(1)}, u32[]{:S(2)}) copy-start(s32[8192]{0:T(1024)S(1)} %gather_fusion.2) | copy-start | bytes 98308
  148.0 4.2 copy-start.4
  148.1 4.0 copy-start.5
  172.4 1.9 copy-start.6
  181.3 292.2 %all-to-all-start = ((f32[64,12,2,512]{3,2,1,0:T(2,128)}), f32[64,12,2,512]{3,2,1,0:T(2,128)S(1)}, u32[]{:S(2)}, u32[]{:S(2)}) async-start(f32[64,12,2,512]{3,2,1,0:T(2,128)} %copy.192), calls=%async_computation | async-start | bytes 6291456 | tf_op jit(solution)/shard_map/all_to_all | solution.py:146
  201.6 4.9 copy-start.8
  482.5 1.7 copy-start.1
  544.9 3.9 collective-permute-start.2
  546.7 4.4 collective-permute-start.3
  552.7 10.2 %all-to-all-start.1 = ((f32[4,166,128]{2,1,0:T(8,128)}), f32[4,166,128]{2,1,0:T(8,128)S(1)}, u32[]{:S(2)}, u32[]{:S(2)}) async-start(f32[4,166,128]{2,1,0:T(8,128)} %broadcast_in_dim.129), calls=%async_computation.1 | async-start | bytes 688128 | tf_op jit(solution)/shard_map/all_to_all | solution.py:38
  612.0 8.0 %copy-start.3 = (s32[128,4]{1,0:T(8,128)S(1)}, s32[128,4]{1,0:T(8,128)}, u32[]{:S(2)}) copy-start(s32[128,4]{1,0:T(8,128)} %get-tuple-element.107) | copy-start | bytes 6148
  612.0 45.8 %all-to-all-start.3 = ((f32[32,2,1,12,512]{4,1,3,2,0:T(2,128)}), f32[32,2,1,12,512]{4,1,3,2,0:T(2,128)}, u32[]{:S(2)}, u32[]{:S(2)}) async-start(f32[32,2,1,12,512]{4,1,3,2,0:T(2,128)} %copy.201), calls=%async_computation.3 | async-start | bytes 3145728 | tf_op jit(solution)/shard_map/all_to_all | solution.py:61
where the time goes:
time: 678 us; the launch traced here: 666 us
  local copies, waits for them, and re-layouts  523 us (77%)
  waiting for transfers between devices  44.8 us (7%)
  starting transfers between devices  34.3 us (5%)
  other arithmetic  34.3 us (5%)
  matrix products  20.2 us (3%)
  blocking collectives  8.29 us (1%)
    scatter x1, local copies, waits for them, and re-layouts, body(): slot_plane = jnp.zeros((slot_total,), jnp.int32).at[slot_flat].set(source...  120 us
    scatter x1, local copies, waits for them, and re-layouts, body(): slot_func = jnp.full((slot_total,), -1, jnp.int32).at[slot_flat].set(sour...  120 us
    gather x14, local copies, waits for them, and re-layouts, body(): jnp.searchsorted(offsets, jnp.arange(planes + 1, dtype=jnp.int32), side='...  86.4 us
    gather x2, local copies, waits for them, and re-layouts, to_band(): jnp.take_along_axis(gram_block, jnp.clip(col_ids, 0, width - 1), axis=1)  52.4 us
    gather x1, local copies, waits for them, and re-layouts, body(): source_planes = (offsets[source_ids][..., None] + piece_range) % planes  45.5 us
    all_to_all x1, waiting for transfers between devices, exchange_in_order(): lax.all_to_all(tiles, axes[k], split_axis=k, concat_axis=k, tiled=True)  37.7 us
    gather x4, local copies, waits for them, and re-layouts, from_band(): return jnp.take_along_axis(band_rows, index_map, axis=1)  29.1 us
    add x5, local copies, waits for them, and re-layouts, body(): source_planes = (offsets[source_ids][..., None] + piece_range) % planes  14.1 us
  transfers between devices with their start and end apart: 7, of which 3 were waited for; matrix products, arithmetic and copies ran while one was open for 65% of the time, Pallas kernels for 0%

commit v1 on v0

v1 whole, which is shorter than its diff:
```python
import jax
import jax.numpy as jnp
from jax import lax
from jax.experimental import pallas as pl
from jax.experimental.pallas import tpu as pltpu
from jax.sharding import PartitionSpec as P

PB = 4
ROWS = 4
CZ = 128
OWN = 128
HALF = 64
HALO = 48
WIDE = 256
CELLS = ROWS * CZ
BOX = PB * ROWS
PENALTY = 0.5
VOLUME = 1.0 / (PB * 16 * CZ)
VMEM = pltpu.CompilerParams(vmem_limit_bytes=40 * 1024 * 1024)


def split(x):
    hi = x.astype(jnp.bfloat16)
    lo = (x - hi.astype(jnp.float32)).astype(jnp.bfloat16)
    return hi, lo


def own_rows(ref, first, step):
    return jnp.concatenate(
        [ref[pl.ds(par * step + first, HALF, stride=2 * step), :] for par in range(2)], axis=0
    )


def potential_kernel(starts, potential, out):
    planes = potential.shape[0]

    def one(m, carry):
        first = starts[m]
        for p in range(PB):
            plane = first + p
            plane = jnp.where(plane >= planes, plane - planes, plane)
            out[m * PB + p] = potential[plane]
        return carry

    lax.fori_loop(0, OWN, one, 0, unroll=4)


def difference(own_start, wide_start, planes):
    d = wide_start[...] - own_start[...]
    d = jnp.where(d >= planes // 2, d - planes, d)
    return jnp.where(d < -(planes // 2), d + planes, d)


def dot_t(a, b):
    return lax.dot_general(a, b, (((1,), (1,)), ((), ())), preferred_element_type=jnp.float32)


def gram_kernel(
    planes, x, low, high, y_before, y_after, pot, own_start, wide_start,
    band, image, bh, bl, fh, fl, gh, gl, hh, hl,
):
    lane = lax.broadcasted_iota(jnp.int32, (OWN, CZ), 1)
    zero = jnp.zeros((16, CELLS), jnp.bfloat16)
    for q in range(PB):
        for ref in (bh, bl):
            ref[q * WIDE : q * WIDE + 16, :] = zero
            ref[q * WIDE + 240 : q * WIDE + 256, :] = zero
        for y in range(ROWS):
            cols = slice(y * CZ, (y + 1) * CZ)
            for ref, at in ((low, 16), (high, 192)):
                hi, lo = split(ref[pl.ds(q * ROWS + y, HALO, stride=BOX), :])
                bh[q * WIDE + at : q * WIDE + at + HALO, cols] = hi
                bl[q * WIDE + at : q * WIDE + at + HALO, cols] = lo
    for y in range(ROWS):
        cols = slice(y * CZ, (y + 1) * CZ)
        phi = [own_rows(x, p * ROWS + y, BOX) for p in range(PB)]
        acted = []
        for p in range(PB):
            hi, lo = split(phi[p])
            bh[p * WIDE + HALF : p * WIDE + HALF + OWN, cols] = hi
            bl[p * WIDE + HALF : p * WIDE + HALF + OWN, cols] = lo
            up = own_rows(y_before, p, PB) if y == 0 else own_rows(x, p * ROWS + y - 1, BOX)
            down = own_rows(y_after, p, PB) if y == ROWS - 1 else own_rows(x, p * ROWS + y + 1, BOX)
            left = jnp.where(lane == 0, 0.0, pltpu.roll(phi[p], 1, 1))
            right = jnp.where(lane == CZ - 1, 0.0, pltpu.roll(phi[p], CZ - 1, 1))
            acted.append(
                (3.0 - PENALTY + own_rows(pot, p * ROWS + y, BOX)) * phi[p]
                - 0.5 * (up + down + left + right)
            )
        half = [-0.5 * v for v in phi]
        full = [half[0]]
        for p in range(PB):
            v = acted[p]
            if p > 0:
                v = v + half[p - 1]
            if p < PB - 1:
                v = v + half[p + 1]
            image[(p * ROWS + y) * OWN : (p * ROWS + y + 1) * OWN, :] = v
            full.append(v)
        full.append(half[PB - 1])
        for k, v in enumerate(full):
            hi, lo = split(v)
            fh[k * OWN : (k + 1) * OWN, cols] = hi
            fl[k * OWN : (k + 1) * OWN, cols] = lo
        for k in range(3):
            p = k + 1
            v = acted[p] if p == PB - 1 else acted[p] + half[p + 1]
            hi, lo = split(v)
            gh[k * OWN : (k + 1) * OWN, cols] = hi
            gl[k * OWN : (k + 1) * OWN, cols] = lo
            p = k
            v = acted[p] if p == 0 else acted[p] + half[p - 1]
            hi, lo = split(v)
            hh[k * OWN : (k + 1) * OWN, cols] = hi
            hl[k * OWN : (k + 1) * OWN, cols] = lo
    apart = difference(own_start, wide_start, planes)
    total = jnp.zeros((OWN, WIDE), jnp.float32)
    pieces = {
        0: ((fh, fl, 0, 2, -1), (gh, gl, 0, 3, 1)),
        1: ((fh, fl, 0, 6, -1),),
        2: ((fh, fl, 0, 6, -1),),
        3: ((hh, hl, 0, 3, 0), (fh, fl, 4, 2, 3)),
    }
    for q in range(PB):
        right_hi = bh[q * WIDE : (q + 1) * WIDE, :]
        right_lo = bl[q * WIDE : (q + 1) * WIDE, :]
        for hi, lo, at, count, first in pieces[q]:
            rows = slice(at * OWN, (at + count) * OWN)
            r = dot_t(hi[rows, :], right_hi) + dot_t(hi[rows, :], right_lo)
            r = r + dot_t(lo[rows, :], right_hi)
            for k in range(count):
                total = total + jnp.where(
                    apart == first + k - q, r[k * OWN : (k + 1) * OWN, :], 0.0
                )
    total = total * VOLUME
    for b in range(4):
        band[32 * b : 32 * b + 32, :] = total[32 * b : 32 * b + 32, 32 * b + 16 : 32 * b + 144]


def update_kernel(
    planes, b0, b1, b2, b3, image, bh, bl, own_start, wide_start, out, wh, wl, wide
):
    band = b0[...] + b1[...] + b2[...] + b3[...]
    for b in range(4):
        parts = [band[32 * b : 32 * b + 32, :]]
        before, after = 32 * b + 16, 112 - 32 * b
        parts = [jnp.zeros((32, before), jnp.float32), *parts, jnp.zeros((32, after), jnp.float32)]
        wide[32 * b : 32 * b + 32, :] = jnp.concatenate(parts, axis=1)
    mixing = wide[...]
    apart = difference(own_start, wide_start, planes)
    for d in range(1 - PB, PB):
        hi, lo = split(jnp.where(apart == d, mixing, 0.0))
        for p in range(PB):
            q = p - d
            if 0 <= q < PB:
                wh[p * OWN : (p + 1) * OWN, q * WIDE : (q + 1) * WIDE] = hi
                wl[p * OWN : (p + 1) * OWN, q * WIDE : (q + 1) * WIDE] = lo
    def dot(a, b):
        return jnp.dot(a, b, preferred_element_type=jnp.float32)

    r = dot(wh[...], bh[...]) + dot(wh[...], bl[...]) + dot(wl[...], bh[...])
    for p in range(PB):
        for y in range(ROWS):
            v = image[(p * ROWS + y) * OWN : (p * ROWS + y + 1) * OWN, :]
            v = v - r[p * OWN : (p + 1) * OWN, y * CZ : (y + 1) * CZ]
            for par in range(2):
                out[pl.ds(par * BOX + p * ROWS + y, HALF, stride=2 * BOX), :] = v[
                    par * HALF : (par + 1) * HALF
                ]


def shifted(x, axis, step, closed):
    n = lax.axis_size(axis)
    return lax.ppermute(
        x, axis, [(i, (i + step) % n) for i in range(n) if closed or 0 <= i + step < n]
    )


def body(coeffs, offsets, potential):
    peers = lax.axis_size("fn")
    position = lax.axis_index("fn")
    planes = potential.shape[0]
    padded = jnp.concatenate([offsets[-HALF:], offsets, offsets[:HALF]])
    wide_start = lax.dynamic_slice(padded, (position * OWN,), (WIDE,))
    own_start = wide_start[HALF : HALF + OWN]
    by_block = own_start.reshape(2, HALF).T.reshape(OWN)
    wide_start = wide_start[None, :]
    own_start = own_start[:, None]
    f32, bf16 = jnp.float32, jnp.bfloat16
    sds = jax.ShapeDtypeStruct

    pot = pl.pallas_call(
        potential_kernel,
        out_shape=sds((OWN * PB, ROWS, CZ), f32),
        in_specs=[
            pl.BlockSpec(memory_space=pltpu.SMEM),
            pl.BlockSpec(memory_space=pltpu.VMEM),
        ],
        out_specs=pl.BlockSpec(memory_space=pltpu.VMEM),
        compiler_params=VMEM,
        cost_estimate=pl.CostEstimate(flops=0, bytes_accessed=4 << 20, transcendentals=0),
        name="box_potential",
    )(by_block, potential)
    pot = pot.reshape(OWN * BOX, CZ)

    x = lax.all_to_all(
        coeffs.reshape(peers, 2 * BOX, CZ), "fn", split_axis=0, concat_axis=0, tiled=True
    )
    boxes = x.reshape(HALF, 2, BOX, CZ)
    rows = x.reshape(OWN * PB, ROWS, CZ)
    y_before = shifted(rows[:, ROWS - 1], "sub", 1, False)
    y_after = shifted(rows[:, 0], "sub", -1, False)
    low = shifted(boxes[HALF - HALO :, 1].reshape(HALO * BOX, CZ), "fn", 1, True)
    high = shifted(boxes[:HALO, 0].reshape(HALO * BOX, CZ), "fn", -1, True)

    band, image, bh, bl = pl.pallas_call(
        lambda *refs: gram_kernel(planes, *refs),
        out_shape=(
            sds((OWN, CZ), f32),
            sds((BOX * OWN, CZ), f32),
            sds((PB * WIDE, CELLS), bf16),
            sds((PB * WIDE, CELLS), bf16),
        ),
        scratch_shapes=[
            pltpu.VMEM((6 * OWN, CELLS), bf16),
            pltpu.VMEM((6 * OWN, CELLS), bf16),
            pltpu.VMEM((3 * OWN, CELLS), bf16),
            pltpu.VMEM((3 * OWN, CELLS), bf16),
            pltpu.VMEM((3 * OWN, CELLS), bf16),
            pltpu.VMEM((3 * OWN, CELLS), bf16),
        ],
        compiler_params=VMEM,
        cost_estimate=pl.CostEstimate(
            flops=3 << 30, bytes_accessed=8 << 20, transcendentals=0
        ),
        name="band",
    )(x.reshape(OWN * BOX, CZ), low, high, y_before, y_after, pot, own_start, wide_start)

    bands = [band] + [shifted(band, "sub", k, True) for k in (1, 2, 3)]
    gradient = pl.pallas_call(
        lambda *refs: update_kernel(planes, *refs),
        out_shape=sds((OWN * BOX, CZ), f32),
        scratch_shapes=[
            pltpu.VMEM((PB * OWN, PB * WIDE), bf16),
            pltpu.VMEM((PB * OWN, PB * WIDE), bf16),
            pltpu.VMEM((OWN, WIDE), f32),
        ],
        compiler_params=VMEM,
        cost_estimate=pl.CostEstimate(
            flops=2 << 30, bytes_accessed=5 << 20, transcendentals=0
        ),
        name="gradient",
    )(*bands, image, bh, bl, own_start, wide_start)
    back = lax.all_to_all(
        gradient.reshape(peers, 2 * BOX, CZ), "fn", split_axis=0, concat_axis=0, tiled=True
    )
    return back.reshape(coeffs.shape)


def solution(mesh):
    return jax.shard_map(
        body,
        mesh=mesh,
        in_specs=(P("fn", None, "sub", None), P(), P(None, "sub", None)),
        out_specs=P("fn", None, "sub", None),
        check_vma=False,
    )
```

time: 678 us -> 115 us (0.17); the launches traced: 666 us -> 115 us
  local copies, waits for them, and re-layouts: 523 us -> 3.85 us
  blocking collectives: 8.29 us -> 77.7 us
  waiting for transfers between devices: 44.8 us -> 9.83 us
  other arithmetic: 34.3 us -> 0 us
  starting transfers between devices: 34.3 us -> 12.5 us
  matrix products: 20.2 us -> 0 us
  Pallas kernels: 0 us -> 10.6 us
    scatter x2 -> x0, local copies, waits for them, and re-layouts: 241 us -> none  [the longest x1 120 us: body(): slot_plane = jnp.zeros((slot_total,), jnp.int32).at[slot_flat].set(source...]
    gather x33 -> x0, local copies, waits for them, and re-layouts: 223 us -> none  [the longest x14 86.4 us: body(): jnp.searchsorted(offsets, jnp.arange(planes + 1, dtype=jnp.int32), side='...]
    all_to_all x1 -> x2, blocking collectives: 8.29 us -> 77.7 us  [the longest x1 41.1 us: body(): lax.all_to_all(coeffs.reshape(peers, 2 * BOX, CZ), 'fn', split_axis=0, co...]
    all_to_all x3 -> x0, waiting for transfers between devices: 43.2 us -> none  [the longest x1 37.7 us: exchange_in_order(): lax.all_to_all(tiles, axes[k], split_axis=k, concat_axis=k, tiled=True)]
    all_to_all x3 -> x0, starting transfers between devices: 25.6 us -> none  [the longest x1 13.4 us: body(): lax.all_to_all(send_buffer.reshape(peer_count, capacity, 2, cell_count),...]
    dot_general x7 -> x0, matrix products: 20.2 us -> none  [the longest x3 10.9 us: select_rows(): return jnp.dot(matrix, data, precision=highest)]
    select_n x40 -> x0, other arithmetic: 16.5 us -> none  [the longest x1 9.96 us: body(): jnp.where(slot_live, local_plane * KMAX + slot_in_plane, slab_planes * KMAX)]
    add x16 -> x0, local copies, waits for them, and re-layouts: 15 us -> none  [the longest x5 14.1 us: body(): source_planes = (offsets[source_ids][..., None] + piece_range) % planes]
  transfers between devices with their start and end apart: 7 -> 7, of which waited for: 3 -> 6; matrix products, arithmetic and copies ran while one was open for 65% -> 1% of each run, Pallas kernels for 0% -> 1%
where the time goes in v1:
time: 115 us
  blocking collectives  77.7 us (68%)
  starting transfers between devices  12.5 us (11%)
  Pallas kernels  10.6 us (9%)
  waiting for transfers between devices  9.83 us (9%)
  local copies, waits for them, and re-layouts  3.85 us (3%)
    all_to_all x1, blocking collectives, body(): lax.all_to_all(coeffs.reshape(peers, 2 * BOX, CZ), 'fn', split_axis=0, co...  41.1 us
    all_to_all x1, blocking collectives, body(): lax.all_to_all(gradient.reshape(peers, 2 * BOX, CZ), 'fn', split_axis=0,...  36.6 us
    ppermute x7, starting transfers between devices, shifted(): lax.ppermute(x, axis, [(i, (i + step) % n) for i in range(n) if closed or...  12.5 us
    ppermute x7, waiting for transfers between devices, shifted(): lax.ppermute(x, axis, [(i, (i + step) % n) for i in range(n) if closed or...  9.83 us
    pallas_call x1, Pallas kernels, body(): pl.pallas_call(lambda *refs: gram_kernel(planes, *refs), out_shape=(sds((...  6.56 us
    pallas_call x1, Pallas kernels, body(): pl.pallas_call(lambda *refs: update_kernel(planes, *refs), out_shape=sds(...  2.48 us
  transfers between devices with their start and end apart: 7, of which 6 were waited for; matrix products, arithmetic and copies ran while one was open for 1% of the time, Pallas kernels for 1%

profile of v1, /device:TPU:1, one launch (start us, length us, event | category | flops | bytes accessed | tf_op | source)
XLA Modules:
  0.0 114.5 jit_solution(5292758402584364708)
XLA Ops:
  0.0 41.1 %all_to_all.10 = f32[64,32,128]{2,1,0:T(8,128)S(1)} all-to-all(f32[64,32,128]{2,1,0:T(8,128)} %bitcast.27), channel_id=1, replica_groups=mesh['fn'=64,'sub'=4] {'fn'}, dimensions={0} | all-to-all | bytes 2097152 | tf_op jit(solution)/shard_map/all_to_all | solution.py:206
  41.1 1.2 %fusion = (f32[512,1,128]{2,1,0:T(1,128)}, f32[512,1,128]{2,1,0:T(1,128)}) fusion(f32[512,4,128]{2,1,0:T(4,128)S(1)} %bitcast.19), kind=kLoop, calls=%fused_computation.1 | loop fusion | bytes 1048576 | tf_op jit(solution)/shard_map/slice | solution.py:212
  42.3 3.2 %collective-permute-start.2 = (f32[512,128]{1,0:T(8,128)}, f32[512,128]{1,0:T(8,128)S(1)}, u32[]{:S(2)}, u32[]{:S(2)}) collective-permute-start(f32[512,128]{1,0:T(8,128)} %bitcast.6), channel_id=1, source_target_pairs={{0,1},{1,2},{2,3},{4,5},{5,6},{6,7},{8,9},{9,10},{10,11},{12,13},{... | collective-permute-start | bytes 786440 | tf_op jit(solution)/shard_map/ppermute | solution.py:174
  45.5 1.3 %collective-permute-start.3 = (f32[512,128]{1,0:T(8,128)}, f32[512,128]{1,0:T(8,128)}, u32[]{:S(2)}, u32[]{:S(2)}) collective-permute-start(f32[512,128]{1,0:T(8,128)} %bitcast.7), channel_id=1, source_target_pairs={{1,0},{2,1},{3,2},{5,4},{6,5},{7,6},{9,8},{10,9},{11,10},{13,12},{... | collective-permute-start | bytes 786440 | tf_op jit(solution)/shard_map/ppermute | solution.py:174
  46.8 0.9 fusion.1
  47.7 2.7 %collective-permute-start = (f32[768,128]{1,0:T(8,128)}, f32[768,128]{1,0:T(8,128)}, u32[]{:S(2)}, u32[]{:S(2)}) collective-permute-start(f32[768,128]{1,0:T(8,128)} %bitcast.3), channel_id=1, source_target_pairs={{0,4},{4,8},{8,12},{12,16},{16,20},{20,24},{24,28},{28,32},{32,36}... | collective-permute-start | bytes 1179656 | tf_op jit(solution)/shard_map/ppermute | solution.py:174
  50.5 0.0 collective-permute-start.1
  50.5 0.0 copy-done.1
  50.5 0.1 fusion.2
  50.5 0.1 concatenate.3
  50.6 0.1 dynamic_slice.3
  50.7 0.1 slice_bitcast_fusion
  50.8 0.1 reshape.39
  50.9 0.1 copy.9
  51.0 0.1 reshape.40.starts
  51.1 0.1 copy.10.refs_6_.refs_7_
  51.2 0.0 copy-done
  51.2 1.6 %box_potential.1 = f32[512,4,128]{2,1,0:T(4,128)S(1)} custom-call(s32[128]{0:T(128)S(1)} %reshape.40.starts, f32[1024,4,128]{2,1,0:T(4,128)S(1)} %copy-done), custom_call_target="tpu_custom_call" | custom-call | bytes 4194304 | tf_op jit(solution)/shard_map/box_potential/pallas_call | solution.py:192
  52.8 0.0 collective-permute-done.2.refs_3_
  52.8 1.1 collective-permute-done.3.refs_4_
  53.9 1.6 %collective-permute-done.refs_1_ = f32[768,128]{1,0:T(8,128)} collective-permute-done((f32[768,128]{1,0:T(8,128)}, f32[768,128]{1,0:T(8,128)}, u32[]{:S(2)}, u32[]{:S(2)}) %collective-permute-start) | collective-permute-done | bytes 393248 | tf_op jit(solution)/shard_map/ppermute | solution.py:174
  55.5 2.8 %collective-permute-done.1.refs_2_ = f32[768,128]{1,0:T(8,128)} collective-permute-done((f32[768,128]{1,0:T(8,128)}, f32[768,128]{1,0:T(8,128)}, u32[]{:S(2)}, u32[]{:S(2)}) %collective-permute-start.1) | collective-permute-done | bytes 393248 | tf_op jit(solution)/shard_map/ppermute | solution.py:174
  58.3 6.6 %band.1 = (f32[128,128]{1,0:T(8,128)S(1)}, f32[2048,128]{1,0:T(8,128)S(1)}, bf16[1024,512]{1,0:T(8,128)(2,1)S(1)}, bf16[1024,512]{1,0:T(8,128)(2,1)S(1)}) custom-call(f32[2048,128]{1,0:T(8,128)S(1)} %bitcast.21, f32[768,128]{1,0:T(8,128)} %collective-permute-done.refs_1_, f32[768,128]{1,0:T(8,128)} %collective-permute-done.1.refs_2_, ...), custom_call_target="tpu_custom_call" | custom-call | flops 3221225472 | bytes 8388608 | tf_op jit(solution)/shard_map/band/pallas_call | solution.py:216
  64.8 4.6 %collective-permute-start.6 = (f32[128,128]{1,0:T(8,128)S(1)}, f32[128,128]{1,0:T(8,128)S(1)}, u32[]{:S(2)}, u32[]{:S(2)}) collective-permute-start(f32[128,128]{1,0:T(8,128)S(1)} %get-tuple-element.9.refs_0_), channel_id=1, source_target_pairs={{0,3},{1,0},{2,1},{3,2},{4,7},{5,4},{6,5},{7,6},{8,11},{9,8},{10,9... | collective-permute-start | bytes 196616 | tf_op jit(solution)/shard_map/ppermute | solution.py:174
  69.4 0.0 collective-permute-start.5
  69.4 0.7 collective-permute-start.4
  70.1 0.7 collective-permute-done.6.refs_3_
  70.7 3.4 %collective-permute-done.5.refs_2_ = f32[128,128]{1,0:T(8,128)S(1)} collective-permute-done((f32[128,128]{1,0:T(8,128)S(1)}, f32[128,128]{1,0:T(8,128)S(1)}, u32[]{:S(2)}, u32[]{:S(2)}) %collective-permute-start.5) | collective-permute-done | bytes 65568 | tf_op jit(solution)/shard_map/ppermute | solution.py:174
  74.1 0.3 collective-permute-done.4.refs_1_
  74.4 2.5 %gradient.1 = f32[2048,128]{1,0:T(8,128)S(1)} custom-call(f32[128,128]{1,0:T(8,128)S(1)} %get-tuple-element.9.refs_0_, f32[128,128]{1,0:T(8,128)S(1)} %collective-permute-done.4.refs_1_, f32[128,128]{1,0:T(8,128)S(1)} %collective-permute-done.5.refs_2_, f32[128,128]{1,0:T(8,128)S(1)} %collective-permute-done.6.refs_3_, ...), custom_call_target="tpu_custom_call" | custom-call | flops 2147483648 | bytes 5242880 | tf_op jit(solution)/shard_map/gradient/pallas_call | solution.py:240
  76.9 36.6 %all_to_all.11 = f32[64,32,128]{2,1,0:T(8,128)S(1)} all-to-all(f32[64,32,128]{2,1,0:T(8,128)S(1)} %bitcast.23), channel_id=1, replica_groups=mesh['fn'=64,'sub'=4] {'fn'}, dimensions={0} | all-to-all | bytes 2097152 | tf_op jit(solution)/shard_map/all_to_all | solution.py:254
  113.6 1.0 copy.15
  (2 shorter events, 0.0 us)
Async XLA Ops:
  0.0 50.5 %copy-start.1 = (s32[8192]{0:T(1024)S(1)}, s32[8192]{0:T(1024)}, u32[]{:S(2)}) copy-start(s32[8192]{0:T(1024)} %param.4) | copy-start | bytes 98308
  0.0 51.2 %copy-start = (f32[1024,4,128]{2,1,0:T(4,128)S(1)}, f32[1024,4,128]{2,1,0:T(4,128)}, u32[]{:S(2)}) copy-start(f32[1024,4,128]{2,1,0:T(4,128)} %potential.1) | copy-start | bytes 6291460
  42.3 10.5 %collective-permute-start.2 = (f32[512,128]{1,0:T(8,128)}, f32[512,128]{1,0:T(8,128)S(1)}, u32[]{:S(2)}, u32[]{:S(2)}) collective-permute-start(f32[512,128]{1,0:T(8,128)} %bitcast.6), channel_id=1, source_target_pairs={{0,1},{1,2},{2,3},{4,5},{5,6},{6,7},{8,9},{9,10},{10,11},{12,13},{... | collective-permute-start | bytes 786440 | tf_op jit(solution)/shard_map/ppermute | solution.py:174
  45.5 8.4 %collective-permute-start.3 = (f32[512,128]{1,0:T(8,128)}, f32[512,128]{1,0:T(8,128)}, u32[]{:S(2)}, u32[]{:S(2)}) collective-permute-start(f32[512,128]{1,0:T(8,128)} %bitcast.7), channel_id=1, source_target_pairs={{1,0},{2,1},{3,2},{5,4},{6,5},{7,6},{9,8},{10,9},{11,10},{13,12},{... | collective-permute-start | bytes 786440 | tf_op jit(solution)/shard_map/ppermute | solution.py:174
  47.7 7.8 %collective-permute-start = (f32[768,128]{1,0:T(8,128)}, f32[768,128]{1,0:T(8,128)}, u32[]{:S(2)}, u32[]{:S(2)}) collective-permute-start(f32[768,128]{1,0:T(8,128)} %bitcast.3), channel_id=1, source_target_pairs={{0,4},{4,8},{8,12},{12,16},{16,20},{20,24},{24,28},{28,32},{32,36}... | collective-permute-start | bytes 1179656 | tf_op jit(solution)/shard_map/ppermute | solution.py:174
  50.5 7.8 %collective-permute-start.1 = (f32[768,128]{1,0:T(8,128)}, f32[768,128]{1,0:T(8,128)}, u32[]{:S(2)}, u32[]{:S(2)}) collective-permute-start(f32[768,128]{1,0:T(8,128)} %bitcast.4), channel_id=1, source_target_pairs={{0,252},{4,0},{8,4},{12,8},{16,12},{20,16},{24,20},{28,24},{32,28}... | collective-permute-start | bytes 1179656 | tf_op jit(solution)/shard_map/ppermute | solution.py:174
  64.8 5.9 %collective-permute-start.6 = (f32[128,128]{1,0:T(8,128)S(1)}, f32[128,128]{1,0:T(8,128)S(1)}, u32[]{:S(2)}, u32[]{:S(2)}) collective-permute-start(f32[128,128]{1,0:T(8,128)S(1)} %get-tuple-element.9.refs_0_), channel_id=1, source_target_pairs={{0,3},{1,0},{2,1},{3,2},{4,7},{5,4},{6,5},{7,6},{8,11},{9,8},{10,9... | collective-permute-start | bytes 196616 | tf_op jit(solution)/shard_map/ppermute | solution.py:174
  69.4 4.7 %collective-permute-start.5 = (f32[128,128]{1,0:T(8,128)S(1)}, f32[128,128]{1,0:T(8,128)S(1)}, u32[]{:S(2)}, u32[]{:S(2)}) collective-permute-start(f32[128,128]{1,0:T(8,128)S(1)} %get-tuple-element.9.refs_0_), channel_id=1, source_target_pairs={{0,2},{1,3},{2,0},{3,1},{4,6},{5,7},{6,4},{7,5},{8,10},{9,11},{10,... | collective-permute-start | bytes 196616 | tf_op jit(solution)/shard_map/ppermute | solution.py:174
  69.4 5.0 %collective-permute-start.4 = (f32[128,128]{1,0:T(8,128)S(1)}, f32[128,128]{1,0:T(8,128)S(1)}, u32[]{:S(2)}, u32[]{:S(2)}) collective-permute-start(f32[128,128]{1,0:T(8,128)S(1)} %get-tuple-element.9.refs_0_), channel_id=1, source_target_pairs={{0,1},{1,2},{2,3},{3,0},{4,5},{5,6},{6,7},{7,4},{8,9},{9,10},{10,1... | collective-permute-start | bytes 196616 | tf_op jit(solution)/shard_map/ppermute | solution.py:174

commit v2 on v1

v2 whole, which is shorter than its diff:
```python
import jax
import jax.numpy as jnp
from jax import lax
from jax.experimental import pallas as pl
from jax.experimental.pallas import tpu as pltpu
from jax.sharding import PartitionSpec as P

PB = 4
ROWS = 4
CZ = 128
OWN = 128
HALF = 64
HALO = 48
WIDE = 256
CELLS = ROWS * CZ
BOX = PB * ROWS
PENALTY = 0.5
INNER = (1, 2)
OUTER = (0, 3)
ORDER = INNER + OUTER
VOLUME = 1.0 / (PB * 16 * CZ)


def vmem(mib):
    return pltpu.CompilerParams(vmem_limit_bytes=mib << 20)


def split(x):
    hi = x.astype(jnp.bfloat16)
    lo = (x - hi.astype(jnp.float32)).astype(jnp.bfloat16)
    return hi, lo


def own_rows(ref, first, step):
    return jnp.concatenate(
        [ref[pl.ds(par * step + first, HALF, stride=2 * step), :] for par in range(2)], axis=0
    )


def potential_kernel(starts, potential, out):
    planes = potential.shape[0]

    for par in range(2):

        def one(f, carry):
            first = starts[par * HALF + f]
            for p in range(PB):
                plane = first + p
                plane = jnp.where(plane >= planes, plane - planes, plane)
                out[(f * 2 + par) * PB + p] = potential[plane]
            return carry

        lax.fori_loop(0, HALF, one, 0, unroll=4)


def edge_kernel(x, first, last, low, high):
    rows, at = PB * OWN, lax.axis_index("sub")
    first[...] = jnp.where(at == 0, 0.0, x[pl.ds(0, rows, stride=ROWS), :])
    last[...] = jnp.where(at == lax.axis_size("sub") - 1, 0.0, x[pl.ds(ROWS - 1, rows, stride=ROWS), :])
    for k in range(HALO):
        to = slice(k * BOX, (k + 1) * BOX)
        low_at = (HALF - HALO + k) * 2 * BOX + BOX
        low[to, :] = x[low_at : low_at + BOX, :]
        high[to, :] = x[k * 2 * BOX : k * 2 * BOX + BOX, :]


def difference(own_start, wide_start, planes):
    d = wide_start[...] - own_start[...]
    d = jnp.where(d >= planes // 2, d - planes, d)
    return jnp.where(d < -(planes // 2), d + planes, d)


def dot_t(a, b):
    return lax.dot_general(a, b, (((1,), (1,)), ((), ())), preferred_element_type=jnp.float32)


def put(hi_ref, lo_ref, k, cols, v):
    hi, lo = split(v)
    hi_ref[k * OWN : (k + 1) * OWN, cols] = hi
    lo_ref[k * OWN : (k + 1) * OWN, cols] = lo


def act(x, pot, p, y, phi):
    lane = lax.broadcasted_iota(jnp.int32, (OWN, CZ), 1)
    first = p * ROWS + y
    beside = jnp.where(lane == 0, 0.0, pltpu.roll(phi, 1, 1))
    beside = beside + jnp.where(lane == CZ - 1, 0.0, pltpu.roll(phi, CZ - 1, 1))
    if y > 0:
        beside = beside + own_rows(x, first - 1, BOX)
    if y < ROWS - 1:
        beside = beside + own_rows(x, first + 1, BOX)
    return (3.0 - PENALTY + own_rows(pot, first, BOX)) * phi - 0.5 * beside


def left_sides(at, phi, acted, image, fh, fl, gh, gl, hh, hl):
    cols = slice(at * CZ, (at + 1) * CZ)
    half = [-0.5 * v for v in phi]
    put(fh, fl, 0, cols, half[0])
    put(fh, fl, 5, cols, half[PB - 1])
    for p in range(PB):
        v = acted[p]
        if p > 0:
            v = v + half[p - 1]
        if p < PB - 1:
            v = v + half[p + 1]
        image[(p * 2 + at) * OWN : (p * 2 + at + 1) * OWN, :] = v
        put(fh, fl, p + 1, cols, v)
    for k in range(3):
        p = k + 1
        put(gh, gl, k, cols, acted[p] if p == PB - 1 else acted[p] + half[p + 1])
        put(hh, hl, k, cols, acted[k] if k == 0 else acted[k] + half[k - 1])


def inner_kernel(x, pot_any, bh, bl, image, partial, fh, fl, gh, gl, hh, hl, pot, sem):
    copy = pltpu.make_async_copy(pot_any, pot, sem)
    copy.start()
    for p in range(PB):
        for at, y in enumerate(ORDER):
            cols = slice(at * CZ, (at + 1) * CZ)
            hi, lo = split(own_rows(x, p * ROWS + y, BOX))
            bh[p, :, cols] = hi
            bl[p, :, cols] = lo
    copy.wait()
    for at, y in enumerate(INNER):
        phi = [own_rows(x, p * ROWS + y, BOX) for p in range(PB)]
        acted = [act(x, pot, p, y, phi[p]) for p in range(PB)]
        left_sides(at, phi, acted, image, fh, fl, gh, gl, hh, hl)
    for at, y in enumerate(OUTER):
        for p in range(PB):
            v = act(x, pot, p, y, own_rows(x, p * ROWS + y, BOX))
            partial[(p * 2 + at) * OWN : (p * 2 + at + 1) * OWN, :] = v


def band_kernel(
    planes, x, low, high, y_before, y_after, partial, own_start, wide_start, own_bh, own_bl,
    fh_in, fl_in, gh_in, gl_in, hh_in, hl_in,
    band, image, bh, bl, fh, fl, gh, gl, hh, hl,
):
    for at, (y, beyond) in enumerate(zip(OUTER, (y_before, y_after))):
        phi = [own_rows(x, p * ROWS + y, BOX) for p in range(PB)]
        acted = [
            partial[(p * 2 + at) * OWN : (p * 2 + at + 1) * OWN, :] - 0.5 * own_rows(beyond, p, PB)
            for p in range(PB)
        ]
        left_sides(at, phi, acted, image, fh, fl, gh, gl, hh, hl)
    zero = jnp.zeros((16, CELLS), jnp.bfloat16)
    for q in range(PB):
        for ref, own in ((bh, own_bh), (bl, own_bl)):
            ref[q, 0:16, :] = zero
            ref[q, HALF : HALF + OWN, :] = own[q]
            ref[q, WIDE - 16 :, :] = zero
        for at, y in enumerate(ORDER):
            cols = slice(at * CZ, (at + 1) * CZ)
            for ref, to in ((low, 16), (high, HALF + OWN)):
                hi, lo = split(ref[pl.ds(q * ROWS + y, HALO, stride=BOX), :])
                bh[q, to : to + HALO, cols] = hi
                bl[q, to : to + HALO, cols] = lo
    apart = difference(own_start, wide_start, planes)
    total = jnp.zeros((OWN, WIDE), jnp.float32)
    full = ((fh_in, fl_in), (fh, fl))
    pieces = {
        0: ((full, 0, 2, -1), (((gh_in, gl_in), (gh, gl)), 0, 3, 1)),
        1: ((full, 0, 6, -1),),
        2: ((full, 0, 6, -1),),
        3: ((((hh_in, hl_in), (hh, hl)), 0, 3, 0), (full, 4, 2, 3)),
    }
    for q in range(PB):
        for sides, at, count, first in pieces[q]:
            rows = slice(at * OWN, (at + count) * OWN)
            r = None
            for side, (hi, lo) in enumerate(sides):
                cols = slice(side * 2 * CZ, (side + 1) * 2 * CZ)
                right_hi, right_lo = bh[q, :, cols], bl[q, :, cols]
                v = dot_t(hi[rows, :], right_hi) + dot_t(hi[rows, :], right_lo)
                v = v + dot_t(lo[rows, :], right_hi)
                r = v if r is None else r + v
            for k in range(count):
                total = total + jnp.where(
                    apart == first + k - q, r[k * OWN : (k + 1) * OWN, :], 0.0
                )
    total = total * VOLUME
    for b in range(4):
        band[32 * b : 32 * b + 32, :] = total[32 * b : 32 * b + 32, 32 * b + 16 : 32 * b + 144]


def update_kernel(
    planes, b0, b1, b2, b3, image_in, image_out, bh, bl, own_start, wide_start, out, wh, wl, wide
):
    band = b0[...] + b1[...] + b2[...] + b3[...]
    for b in range(4):
        parts = [band[32 * b : 32 * b + 32, :]]
        before, after = 32 * b + 16, 112 - 32 * b
        parts = [jnp.zeros((32, before), jnp.float32), *parts, jnp.zeros((32, after), jnp.float32)]
        wide[32 * b : 32 * b + 32, :] = jnp.concatenate(parts, axis=1)
    mixing = wide[...]
    apart = difference(own_start, wide_start, planes)
    for d in range(1 - PB, PB):
        hi, lo = split(jnp.where(apart == d, mixing, 0.0))
        for p in range(PB):
            q = p - d
            if 0 <= q < PB:
                wh[p * OWN : (p + 1) * OWN, q * WIDE : (q + 1) * WIDE] = hi
                wl[p * OWN : (p + 1) * OWN, q * WIDE : (q + 1) * WIDE] = lo
    def dot(a, b):
        return jnp.dot(a, b, preferred_element_type=jnp.float32)

    r = dot(wh[...], bh[...]) + dot(wh[...], bl[...]) + dot(wl[...], bh[...])
    for p in range(PB):
        for at, y in enumerate(ORDER):
            image = (image_in, image_out)[at // 2]
            first = (p * 2 + at % 2) * OWN
            v = image[first : first + OWN, :]
            v = v - r[p * OWN : (p + 1) * OWN, at * CZ : (at + 1) * CZ]
            for par in range(2):
                out[pl.ds(par * BOX + p * ROWS + y, HALF, stride=2 * BOX), :] = v[
                    par * HALF : (par + 1) * HALF
                ]


def shifted(x, axis, step):
    n = lax.axis_size(axis)
    return lax.ppermute(x, axis, [(i, (i + step) % n) for i in range(n)])


def body(coeffs, offsets, potential):
    peers = lax.axis_size("fn")
    position = lax.axis_index("fn")
    planes = potential.shape[0]
    padded = jnp.concatenate([offsets[-HALF:], offsets, offsets[:HALF]])
    wide_start = lax.dynamic_slice(padded, (position * OWN,), (WIDE,))
    own_start = wide_start[HALF : HALF + OWN]
    f32, bf16 = jnp.float32, jnp.bfloat16
    sds = jax.ShapeDtypeStruct

    def cost(flops, size):
        return pl.CostEstimate(flops=flops, bytes_accessed=size, transcendentals=0)

    pot = pl.pallas_call(
        potential_kernel,
        out_shape=sds((OWN * PB, ROWS, CZ), f32),
        in_specs=[
            pl.BlockSpec(memory_space=pltpu.SMEM),
            pl.BlockSpec(memory_space=pltpu.VMEM),
        ],
        compiler_params=vmem(10),
        cost_estimate=cost(0, 4 << 20),
        name="box_potential",
    )(own_start, potential)
    pot = pot.reshape(OWN * BOX, CZ)
    wide_start = wide_start[None, :]
    own_start = own_start[:, None]

    x = lax.all_to_all(
        coeffs.reshape(peers, 2 * BOX, CZ), "fn", split_axis=0, concat_axis=0, tiled=True
    )
    x, pot, own_start, wide_start = lax.optimization_barrier((x, pot, own_start, wide_start))
    x = x.reshape(OWN * BOX, CZ)
    edge, halo = sds((OWN * PB, CZ), f32), sds((HALO * BOX, CZ), f32)
    first, last, low, high = pl.pallas_call(
        edge_kernel,
        out_shape=(edge, edge, halo, halo),
        compiler_params=vmem(10),
        cost_estimate=cost(0, 2 << 20),
        name="edges",
    )(x)
    y_before = shifted(last, "sub", 1)
    y_after = shifted(first, "sub", -1)
    low = shifted(low, "fn", 1)
    high = shifted(high, "fn", -1)

    image = sds((PB * 2 * OWN, CZ), f32)
    left = [sds((n * OWN, 2 * CZ), bf16) for n in (6, 6, 3, 3, 3, 3)]
    own_bh, own_bl, image_in, partial, *ready = pl.pallas_call(
        inner_kernel,
        out_shape=(sds((PB, OWN, CELLS), bf16), sds((PB, OWN, CELLS), bf16), image, image, *left),
        in_specs=[pl.BlockSpec(memory_space=pltpu.VMEM), pl.BlockSpec(memory_space=pl.ANY)],
        scratch_shapes=[pltpu.VMEM((OWN * BOX, CZ), f32), pltpu.SemaphoreType.DMA],
        compiler_params=vmem(20),
        cost_estimate=cost(1 << 30, 5 << 20),
        name="inner_rows",
    )(x, pot)

    band, image_out, bh, bl = pl.pallas_call(
        lambda *refs: band_kernel(planes, *refs),
        out_shape=(
            sds((OWN, CZ), f32),
            image,
            sds((PB, WIDE, CELLS), bf16),
            sds((PB, WIDE, CELLS), bf16),
        ),
        scratch_shapes=[pltpu.VMEM(v.shape, v.dtype) for v in left],
        compiler_params=vmem(20),
        cost_estimate=cost(3 << 30, 8 << 20),
        name="band",
    )(x, low, high, y_before, y_after, partial, own_start, wide_start, own_bh, own_bl, *ready)

    bands = [band] + [shifted(band, "sub", k) for k in (1, 2, 3)]
    gradient = pl.pallas_call(
        lambda *refs: update_kernel(planes, *refs),
        out_shape=sds((OWN * BOX, CZ), f32),
        scratch_shapes=[
            pltpu.VMEM((PB * OWN, PB * WIDE), bf16),
            pltpu.VMEM((PB * OWN, PB * WIDE), bf16),
            pltpu.VMEM((OWN, WIDE), f32),
        ],
        compiler_params=vmem(20),
        cost_estimate=cost(2 << 30, 5 << 20),
        name="gradient",
    )(
        *bands, image_in, image_out, bh.reshape(PB * WIDE, CELLS), bl.reshape(PB * WIDE, CELLS),
        own_start, wide_start,
    )
    back = lax.all_to_all(
        gradient.reshape(peers, 2, PB, ROWS, CZ), "fn", split_axis=0, concat_axis=0, tiled=True
    )
    return back.reshape(coeffs.shape)


def solution(mesh):
    return jax.shard_map(
        body,
        mesh=mesh,
        in_specs=(P("fn", None, "sub", None), P(), P(None, "sub", None)),
        out_specs=P("fn", None, "sub", None),
        check_vma=False,
    )
```

time: 115 us -> 105 us (0.913)
  blocking collectives: 77.7 us -> 38.1 us
  waiting for transfers between devices: 9.83 us -> 29.4 us
  starting transfers between devices: 12.5 us -> 22.1 us
    all_to_all x2 -> x1, blocking collectives: 77.7 us -> 38.1 us  [body(): lax.all_to_all(gradient.reshape(peers, 2, PB, ROWS, CZ), 'fn', split_axis...]
    all_to_all x0 -> x1, waiting for transfers between devices: none -> 25.1 us  [body(): lax.all_to_all(coeffs.reshape(peers, 2 * BOX, CZ), 'fn', split_axis=0, co...]
    all_to_all x0 -> x1, starting transfers between devices: none -> 13.1 us  [body(): lax.all_to_all(coeffs.reshape(peers, 2 * BOX, CZ), 'fn', split_axis=0, co...]
    ppermute x7, waiting for transfers between devices: 9.83 us -> 4.29 us  [shifted(): return lax.ppermute(x, axis, [(i, (i + step) % n) for i in range(n)])]
    ppermute x7, starting transfers between devices: 12.5 us -> 8.95 us  [shifted(): return lax.ppermute(x, axis, [(i, (i + step) % n) for i in range(n)])]
    unnamed x5 -> x9, local copies, waits for them, and re-layouts: 0.98 us -> 3.16 us
    slice x2 -> x0, local copies, waits for them, and re-layouts: 2.13 us -> none  [the longest x1 1.19 us: body(): y_after = shifted(rows[:, 0], 'sub', -1, False)]
    pallas_call x1 -> x3, Pallas kernels: 6.56 us -> 7.45 us  [the longest x1 3.46 us: body(): pl.pallas_call(inner_kernel, out_shape=(sds((PB, OWN, CELLS), bf16), sds(...]
  transfers between devices with their start and end apart: 7 -> 8, of which waited for: 6 -> 4; matrix products, arithmetic and copies ran while one was open for 1% -> 0% of each run, Pallas kernels for 1% -> 5%
where the time goes in v2:
time: 105 us
  blocking collectives  38.1 us (36%)
  waiting for transfers between devices  29.4 us (28%)
  starting transfers between devices  22.1 us (21%)
  Pallas kernels  11.5 us (11%)
  local copies, waits for them, and re-layouts  3.59 us (3%)
    all_to_all x1, blocking collectives, body(): lax.all_to_all(gradient.reshape(peers, 2, PB, ROWS, CZ), 'fn', split_axis...  38.1 us
    all_to_all x1, waiting for transfers between devices, body(): lax.all_to_all(coeffs.reshape(peers, 2 * BOX, CZ), 'fn', split_axis=0, co...  25.1 us
    all_to_all x1, starting transfers between devices, body(): lax.all_to_all(coeffs.reshape(peers, 2 * BOX, CZ), 'fn', split_axis=0, co...  13.1 us
    ppermute x7, starting transfers between devices, shifted(): return lax.ppermute(x, axis, [(i, (i + step) % n) for i in range(n)])  8.95 us
    ppermute x7, waiting for transfers between devices, shifted(): return lax.ppermute(x, axis, [(i, (i + step) % n) for i in range(n)])  4.29 us
    pallas_call x1, Pallas kernels, body(): pl.pallas_call(inner_kernel, out_shape=(sds((PB, OWN, CELLS), bf16), sds(...  3.46 us
    unnamed x9, local copies, waits for them, and re-layouts  3.16 us
    pallas_call x1, Pallas kernels, body(): pl.pallas_call(lambda *refs: band_kernel(planes, *refs), out_shape=(sds((...  3.1 us
  transfers between devices with their start and end apart: 8, of which 4 were waited for; matrix products, arithmetic and copies ran while one was open for 0% of the time, Pallas kernels for 5%

profile of v2, /device:TPU:1, one launch (start us, length us, event | category | flops | bytes accessed | tf_op | source)
XLA Modules:
  0.0 104.7 jit_solution(12908777607232373514)
XLA Ops:
  0.0 13.1 %all-to-all-start = ((f32[64,32,128]{2,1,0:T(8,128)}), f32[64,32,128]{2,1,0:T(8,128)S(1)}, u32[]{:S(2)}, u32[]{:S(2)}) async-start(f32[64,32,128]{2,1,0:T(8,128)} %bitcast.20), calls=%async_computation | async-start | bytes 2097152 | tf_op jit(solution)/shard_map/all_to_all | solution.py:253
  13.1 0.1 fusion
  13.2 0.1 concatenate.3
  13.3 0.1 dynamic_slice.3
  13.4 0.1 slice_bitcast_fusion
  13.5 0.0 copy-done
  13.5 1.6 %box_potential.1 = f32[512,4,128]{2,1,0:T(4,128)S(1)} custom-call(s32[128]{0:T(128)S(1)} %get-tuple-element.52.starts, f32[1024,4,128]{2,1,0:T(4,128)S(1)} %copy-done), custom_call_target="tpu_custom_call" | custom-call | bytes 4194304 | tf_op jit(solution)/shard_map/box_potential/pallas_call | solution.py:238
  15.0 0.0 copy-start.1
  15.1 1.0 copy-done.1
  16.0 25.1 %all-to-all-done = f32[64,32,128]{2,1,0:T(8,128)S(1)} async-done(((f32[64,32,128]{2,1,0:T(8,128)}), f32[64,32,128]{2,1,0:T(8,128)S(1)}, u32[]{:S(2)}, u32[]{:S(2)}) %all-to-all-start) | async-done | bytes 1048608 | tf_op jit(solution)/shard_map/all_to_all | solution.py:253
  41.1 0.9 edges.1
  42.0 2.4 %collective-permute-start = (f32[768,128]{1,0:T(8,128)S(1)}, f32[768,128]{1,0:T(8,128)S(1)}, u32[]{:S(2)}, u32[]{:S(2)}) collective-permute-start(f32[768,128]{1,0:T(8,128)S(1)} %get-tuple-element.28), channel_id=1, source_target_pairs={{0,4},{4,8},{8,12},{12,16},{16,20},{20,24},{24,28},{28,32},{32,36}... | collective-permute-start | bytes 1179656 | tf_op jit(solution)/shard_map/ppermute | solution.py:222
  44.5 0.0 collective-permute-start.1
  44.5 1.3 %collective-permute-start.2 = (f32[512,128]{1,0:T(8,128)}, f32[512,128]{1,0:T(8,128)S(1)}, u32[]{:S(2)}, u32[]{:S(2)}) collective-permute-start(f32[512,128]{1,0:T(8,128)} %get-tuple-element.30), channel_id=1, source_target_pairs={{0,1},{1,2},{2,3},{3,0},{4,5},{5,6},{6,7},{7,4},{8,9},{9,10},{10,1... | collective-permute-start | bytes 786440 | tf_op jit(solution)/shard_map/ppermute | solution.py:222
  45.8 1.4 %collective-permute-start.3 = (f32[512,128]{1,0:T(8,128)}, f32[512,128]{1,0:T(8,128)S(1)}, u32[]{:S(2)}, u32[]{:S(2)}) collective-permute-start(f32[512,128]{1,0:T(8,128)} %get-tuple-element.31), channel_id=1, source_target_pairs={{0,3},{1,0},{2,1},{3,2},{4,7},{5,4},{6,5},{7,6},{8,11},{9,8},{10,9... | collective-permute-start | bytes 786440 | tf_op jit(solution)/shard_map/ppermute | solution.py:222
  47.2 0.1 copy.4.refs_6_.refs_8_
  47.3 1.2 %copy-done.2 = f32[512,4,128]{2,1,0:T(4,128)S(1)} copy-done((f32[512,4,128]{2,1,0:T(4,128)S(1)}, f32[512,4,128]{2,1,0:T(4,128)}, u32[]{:S(2)}) %copy-start.2) | copy-done | bytes 1048600
  48.5 3.5 %inner_rows.1 = (bf16[4,128,512]{2,1,0:T(8,128)(2,1)S(1)}, bf16[4,128,512]{2,1,0:T(8,128)(2,1)S(1)}, f32[1024,128]{1,0:T(8,128)S(1)}, f32[1024,128]{1,0:T(8,128)...) custom-call(f32[2048,128]{1,0:T(8,128)S(1)} %bitcast.11, ...), custom_call_target="tpu_custom_call" | custom-call | flops 1073741824 | bytes 5242880 | tf_op jit(solution)/shard_map/inner_rows/pallas_call | solution.py:273
  52.0 0.0 collective-permute-done.2.refs_3_
  52.0 0.0 collective-permute-done.3.refs_4_
  52.0 0.0 collective-permute-done.refs_1_
  52.0 0.0 collective-permute-done.1.refs_2_
  52.0 3.1 %band.1 = (f32[128,128]{1,0:T(8,128)S(1)}, f32[1024,128]{1,0:T(8,128)S(1)}, bf16[4,256,512]{2,1,0:T(8,128)(2,1)S(1)}, bf16[4,256,512]{2,1,0:T(8,128)(2,1)S(1)}) custom-call(f32[2048,128]{1,0:T(8,128)S(1)} %bitcast.12, f32[768,128]{1,0:T(8,128)S(1)} %collective-permute-done.refs_1_, f32[768,128]{1,0:T(8,128)S(1)} %collective-permute-done.1.refs_2_, ...), custom_call_target="tpu_custom_call" | custom-call | flops 3221225472 | bytes 8388608 | tf_op jit(solution)/shard_map/band/pallas_call | solution.py:283
  55.1 2.7 %collective-permute-start.6 = (f32[128,128]{1,0:T(8,128)S(1)}, f32[128,128]{1,0:T(8,128)S(1)}, u32[]{:S(2)}, u32[]{:S(2)}) collective-permute-start(f32[128,128]{1,0:T(8,128)S(1)} %get-tuple-element.44.refs_0_), channel_id=1, source_target_pairs={{0,3},{1,0},{2,1},{3,2},{4,7},{5,4},{6,5},{7,6},{8,11},{9,8},{10,9... | collective-permute-start | bytes 196616 | tf_op jit(solution)/shard_map/ppermute | solution.py:222
  57.9 0.3 collective-permute-start.5
  58.2 0.7 collective-permute-start.4
  58.9 0.3 collective-permute-done.6.refs_3_
  59.2 3.4 %collective-permute-done.5.refs_2_ = f32[128,128]{1,0:T(8,128)S(1)} collective-permute-done((f32[128,128]{1,0:T(8,128)S(1)}, f32[128,128]{1,0:T(8,128)S(1)}, u32[]{:S(2)}, u32[]{:S(2)}) %collective-permute-start.5) | collective-permute-done | bytes 65568 | tf_op jit(solution)/shard_map/ppermute | solution.py:222
  62.6 0.6 collective-permute-done.4.refs_1_
  63.2 2.5 %gradient.1 = f32[2048,128]{1,0:T(8,128)S(1)} custom-call(f32[128,128]{1,0:T(8,128)S(1)} %get-tuple-element.44.refs_0_, f32[128,128]{1,0:T(8,128)S(1)} %collective-permute-done.4.refs_1_, f32[128,128]{1,0:T(8,128)S(1)} %collective-permute-done.5.refs_2_, f32[128,128]{1,0:T(8,128)S(1)} %collective-permute-done.6.refs_3_, ...), custom_call_target="tpu_custom_call" | custom-call | flops 2147483648 | bytes 5242880 | tf_op jit(solution)/shard_map/gradient/pallas_call | solution.py:298
  65.7 38.1 %all_to_all.10 = f32[64,2,4,4,128]{4,3,2,1,0:T(4,128)S(1)} all-to-all(f32[64,2,4,4,128]{4,3,2,1,0:T(4,128)S(1)} %bitcast.14), channel_id=1, replica_groups=mesh['fn'=64,'sub'=4] {'fn'}, dimensions={0} | all-to-all | bytes 2097152 | tf_op jit(solution)/shard_map/all_to_all | solution.py:313
  103.7 1.0 copy.7
  (4 shorter events, 0.0 us)
Async XLA Ops:
  0.0 13.1 %copy-start.3 = (s32[8192]{0:T(1024)S(1)}, s32[8192]{0:T(1024)}, u32[]{:S(2)}) copy-start(s32[8192]{0:T(1024)} %param.4) | copy-start | bytes 98308
  0.0 13.5 %copy-start = (f32[1024,4,128]{2,1,0:T(4,128)S(1)}, f32[1024,4,128]{2,1,0:T(4,128)}, u32[]{:S(2)}) copy-start(f32[1024,4,128]{2,1,0:T(4,128)} %potential.1) | copy-start | bytes 6291460
  0.0 41.1 %all-to-all-start = ((f32[64,32,128]{2,1,0:T(8,128)}), f32[64,32,128]{2,1,0:T(8,128)S(1)}, u32[]{:S(2)}, u32[]{:S(2)}) async-start(f32[64,32,128]{2,1,0:T(8,128)} %bitcast.20), calls=%async_computation | async-start | bytes 2097152 | tf_op jit(solution)/shard_map/all_to_all | solution.py:253
  15.0 1.0 copy-start.1
  42.0 10.0 %collective-permute-start = (f32[768,128]{1,0:T(8,128)S(1)}, f32[768,128]{1,0:T(8,128)S(1)}, u32[]{:S(2)}, u32[]{:S(2)}) collective-permute-start(f32[768,128]{1,0:T(8,128)S(1)} %get-tuple-element.28), channel_id=1, source_target_pairs={{0,4},{4,8},{8,12},{12,16},{16,20},{20,24},{24,28},{28,32},{32,36}... | collective-permute-start | bytes 1179656 | tf_op jit(solution)/shard_map/ppermute | solution.py:222
  44.5 7.6 %collective-permute-start.1 = (f32[768,128]{1,0:T(8,128)S(1)}, f32[768,128]{1,0:T(8,128)S(1)}, u32[]{:S(2)}, u32[]{:S(2)}) collective-permute-start(f32[768,128]{1,0:T(8,128)S(1)} %get-tuple-element.29), channel_id=1, source_target_pairs={{0,252},{4,0},{8,4},{12,8},{16,12},{20,16},{24,20},{28,24},{32,28}... | collective-permute-start | bytes 1179656 | tf_op jit(solution)/shard_map/ppermute | solution.py:222
  44.5 7.5 %collective-permute-start.2 = (f32[512,128]{1,0:T(8,128)}, f32[512,128]{1,0:T(8,128)S(1)}, u32[]{:S(2)}, u32[]{:S(2)}) collective-permute-start(f32[512,128]{1,0:T(8,128)} %get-tuple-element.30), channel_id=1, source_target_pairs={{0,1},{1,2},{2,3},{3,0},{4,5},{5,6},{6,7},{7,4},{8,9},{9,10},{10,1... | collective-permute-start | bytes 786440 | tf_op jit(solution)/shard_map/ppermute | solution.py:222
  45.8 6.3 %collective-permute-start.3 = (f32[512,128]{1,0:T(8,128)}, f32[512,128]{1,0:T(8,128)S(1)}, u32[]{:S(2)}, u32[]{:S(2)}) collective-permute-start(f32[512,128]{1,0:T(8,128)} %get-tuple-element.31), channel_id=1, source_target_pairs={{0,3},{1,0},{2,1},{3,2},{4,7},{5,4},{6,5},{7,6},{8,11},{9,8},{10,9... | collective-permute-start | bytes 786440 | tf_op jit(solution)/shard_map/ppermute | solution.py:222
  47.3 1.2 %copy-start.2 = (f32[512,4,128]{2,1,0:T(4,128)S(1)}, f32[512,4,128]{2,1,0:T(4,128)}, u32[]{:S(2)}) copy-start(f32[512,4,128]{2,1,0:T(4,128)} %copy-done.1) | copy-start | bytes 3145732
  55.1 4.1 %collective-permute-start.6 = (f32[128,128]{1,0:T(8,128)S(1)}, f32[128,128]{1,0:T(8,128)S(1)}, u32[]{:S(2)}, u32[]{:S(2)}) collective-permute-start(f32[128,128]{1,0:T(8,128)S(1)} %get-tuple-element.44.refs_0_), channel_id=1, source_target_pairs={{0,3},{1,0},{2,1},{3,2},{4,7},{5,4},{6,5},{7,6},{8,11},{9,8},{10,9... | collective-permute-start | bytes 196616 | tf_op jit(solution)/shard_map/ppermute | solution.py:222
  57.9 4.7 %collective-permute-start.5 = (f32[128,128]{1,0:T(8,128)S(1)}, f32[128,128]{1,0:T(8,128)S(1)}, u32[]{:S(2)}, u32[]{:S(2)}) collective-permute-start(f32[128,128]{1,0:T(8,128)S(1)} %get-tuple-element.44.refs_0_), channel_id=1, source_target_pairs={{0,2},{1,3},{2,0},{3,1},{4,6},{5,7},{6,4},{7,5},{8,10},{9,11},{10,... | collective-permute-start | bytes 196616 | tf_op jit(solution)/shard_map/ppermute | solution.py:222
  58.2 5.0 %collective-permute-start.4 = (f32[128,128]{1,0:T(8,128)S(1)}, f32[128,128]{1,0:T(8,128)S(1)}, u32[]{:S(2)}, u32[]{:S(2)}) collective-permute-start(f32[128,128]{1,0:T(8,128)S(1)} %get-tuple-element.44.refs_0_), channel_id=1, source_target_pairs={{0,1},{1,2},{2,3},{3,0},{4,5},{5,6},{6,7},{7,4},{8,9},{9,10},{10,1... | collective-permute-start | bytes 196616 | tf_op jit(solution)/shard_map/ppermute | solution.py:222

commit v3 on v2

--- a/solution.py
+++ b/solution.py
@@ -18,6 +18,7 @@
 INNER = (1, 2)
 OUTER = (0, 3)
 ORDER = INNER + OUTER
+LINE = 8
 VOLUME = 1.0 / (PB * 16 * CZ)
 
 
@@ -40,23 +41,26 @@
 def potential_kernel(starts, potential, out):
     planes = potential.shape[0]
 
-    for par in range(2):
-
-        def one(f, carry):
-            first = starts[par * HALF + f]
-            for p in range(PB):
-                plane = first + p
-                plane = jnp.where(plane >= planes, plane - planes, plane)
-                out[(f * 2 + par) * PB + p] = potential[plane]
-            return carry
-
-        lax.fori_loop(0, HALF, one, 0, unroll=4)
+    def one(n, carry):
+        first = starts[n]
+        for p in range(PB):
+            plane = first + p
+            plane = jnp.where(plane >= planes, plane - planes, plane)
+            v = potential[plane]
+            for y in range(ROWS):
+                out[pl.ds((p * ROWS + y) * OWN + n, 1), :] = v[y : y + 1, :]
+        return carry
+
+    lax.fori_loop(0, OWN, one, 0, unroll=4)
 
 
 def edge_kernel(x, first, last, low, high):
-    rows, at = PB * OWN, lax.axis_index("sub")
-    first[...] = jnp.where(at == 0, 0.0, x[pl.ds(0, rows, stride=ROWS), :])
-    last[...] = jnp.where(at == lax.axis_size("sub") - 1, 0.0, x[pl.ds(ROWS - 1, rows, stride=ROWS), :])
+    at = lax.axis_index("sub")
+    for p in range(PB):
+        to = slice(p * OWN, (p + 1) * OWN)
+        first[to, :] = jnp.where(at == 0, 0.0, own_rows(x, p * ROWS, BOX))
+        v = own_rows(x, p * ROWS + ROWS - 1, BOX)
+        last[to, :] = jnp.where(at == lax.axis_size("sub") - 1, 0.0, v)
     for k in range(HALO):
         to = slice(k * BOX, (k + 1) * BOX)
         low_at = (HALF - HALO + k) * 2 * BOX + BOX
@@ -74,22 +78,27 @@
     return lax.dot_general(a, b, (((1,), (1,)), ((), ())), preferred_element_type=jnp.float32)
 
 
+def block(ref, p, y):
+    at = (p * ROWS + y) * OWN
+    return ref[at : at + OWN, :]
+
+
 def put(hi_ref, lo_ref, k, cols, v):
     hi, lo = split(v)
     hi_ref[k * OWN : (k + 1) * OWN, cols] = hi
     lo_ref[k * OWN : (k + 1) * OWN, cols] = lo
 
 
-def act(x, pot, p, y, phi):
+def act(xs, pot, p, y):
     lane = lax.broadcasted_iota(jnp.int32, (OWN, CZ), 1)
-    first = p * ROWS + y
+    phi = block(xs, p, y)
     beside = jnp.where(lane == 0, 0.0, pltpu.roll(phi, 1, 1))
     beside = beside + jnp.where(lane == CZ - 1, 0.0, pltpu.roll(phi, CZ - 1, 1))
     if y > 0:
-        beside = beside + own_rows(x, first - 1, BOX)
+        beside = beside + block(xs, p, y - 1)
     if y < ROWS - 1:
-        beside = beside + own_rows(x, first + 1, BOX)
-    return (3.0 - PENALTY + own_rows(pot, first, BOX)) * phi - 0.5 * beside
+        beside = beside + block(xs, p, y + 1)
+    return (3.0 - PENALTY + block(pot, p, y)) * phi - 0.5 * beside
 
 
 def left_sides(at, phi, acted, image, fh, fl, gh, gl, hh, hl):
@@ -111,38 +120,64 @@
         put(hh, hl, k, cols, acted[k] if k == 0 else acted[k] + half[k - 1])
 
 
-def inner_kernel(x, pot_any, bh, bl, image, partial, fh, fl, gh, gl, hh, hl, pot, sem):
+def inner_kernel(x, pot_any, bh, bl, xs, image, partial, fh, fl, gh, gl, hh, hl, pot, sem):
     copy = pltpu.make_async_copy(pot_any, pot, sem)
     copy.start()
     for p in range(PB):
         for at, y in enumerate(ORDER):
             cols = slice(at * CZ, (at + 1) * CZ)
-            hi, lo = split(own_rows(x, p * ROWS + y, BOX))
+            v = own_rows(x, p * ROWS + y, BOX)
+            to = (p * ROWS + y) * OWN
+            xs[to : to + OWN, :] = v
+            hi, lo = split(v)
             bh[p, :, cols] = hi
             bl[p, :, cols] = lo
     copy.wait()
     for at, y in enumerate(INNER):
-        phi = [own_rows(x, p * ROWS + y, BOX) for p in range(PB)]
-        acted = [act(x, pot, p, y, phi[p]) for p in range(PB)]
+        phi = [block(xs, p, y) for p in range(PB)]
+        acted = [act(xs, pot, p, y) for p in range(PB)]
         left_sides(at, phi, acted, image, fh, fl, gh, gl, hh, hl)
     for at, y in enumerate(OUTER):
         for p in range(PB):
-            v = act(x, pot, p, y, own_rows(x, p * ROWS + y, BOX))
-            partial[(p * 2 + at) * OWN : (p * 2 + at + 1) * OWN, :] = v
-
-
-def band_kernel(
-    planes, x, low, high, y_before, y_after, partial, own_start, wide_start, own_bh, own_bl,
-    fh_in, fl_in, gh_in, gl_in, hh_in, hl_in,
-    band, image, bh, bl, fh, fl, gh, gl, hh, hl,
-):
+            partial[(p * 2 + at) * OWN : (p * 2 + at + 1) * OWN, :] = act(xs, pot, p, y)
+
+
+def outer_rows(xs, y_before, y_after, partial, image, fh, fl, gh, gl, hh, hl):
     for at, (y, beyond) in enumerate(zip(OUTER, (y_before, y_after))):
-        phi = [own_rows(x, p * ROWS + y, BOX) for p in range(PB)]
+        phi = [block(xs, p, y) for p in range(PB)]
         acted = [
-            partial[(p * 2 + at) * OWN : (p * 2 + at + 1) * OWN, :] - 0.5 * own_rows(beyond, p, PB)
+            partial[(p * 2 + at) * OWN : (p * 2 + at + 1) * OWN, :]
+            - 0.5 * beyond[p * OWN : (p + 1) * OWN, :]
             for p in range(PB)
         ]
         left_sides(at, phi, acted, image, fh, fl, gh, gl, hh, hl)
+
+
+def products(total, apart, bh, bl, side, fh, fl, gh, gl, hh, hl):
+    cols = slice(side * 2 * CZ, (side + 1) * 2 * CZ)
+    pieces = {
+        0: ((fh, fl, 0, 2, -1), (gh, gl, 0, 3, 1)),
+        1: ((fh, fl, 0, 6, -1),),
+        2: ((fh, fl, 0, 6, -1),),
+        3: ((hh, hl, 0, 3, 0), (fh, fl, 4, 2, 3)),
+    }
+    for q in range(PB):
+        right_hi, right_lo = bh[q, :, cols], bl[q, :, cols]
+        for hi, lo, at, count, first in pieces[q]:
+            rows = slice(at * OWN, (at + count) * OWN)
+            r = dot_t(hi[rows, :], right_hi) + dot_t(hi[rows, :], right_lo)
+            r = r + dot_t(lo[rows, :], right_hi)
+            for k in range(count):
+                total = total + jnp.where(
+                    apart == first + k - q, r[k * OWN : (k + 1) * OWN, :], 0.0
+                )
+    return total
+
+
+def inner_band_kernel(
+    planes, low, high, own_start, wide_start, own_bh, own_bl, fh, fl, gh, gl, hh, hl,
+    bh, bl, total,
+):
     zero = jnp.zeros((16, CELLS), jnp.bfloat16)
     for q in range(PB):
         for ref, own in ((bh, own_bh), (bl, own_bl)):
@@ -156,29 +191,17 @@
                 bh[q, to : to + HALO, cols] = hi
                 bl[q, to : to + HALO, cols] = lo
     apart = difference(own_start, wide_start, planes)
-    total = jnp.zeros((OWN, WIDE), jnp.float32)
-    full = ((fh_in, fl_in), (fh, fl))
-    pieces = {
-        0: ((full, 0, 2, -1), (((gh_in, gl_in), (gh, gl)), 0, 3, 1)),
-        1: ((full, 0, 6, -1),),
-        2: ((full, 0, 6, -1),),
-        3: ((((hh_in, hl_in), (hh, hl)), 0, 3, 0), (full, 4, 2, 3)),
-    }
-    for q in range(PB):
-        for sides, at, count, first in pieces[q]:
-            rows = slice(at * OWN, (at + count) * OWN)
-            r = None
-            for side, (hi, lo) in enumerate(sides):
-                cols = slice(side * 2 * CZ, (side + 1) * 2 * CZ)
-                right_hi, right_lo = bh[q, :, cols], bl[q, :, cols]
-                v = dot_t(hi[rows, :], right_hi) + dot_t(hi[rows, :], right_lo)
-                v = v + dot_t(lo[rows, :], right_hi)
-                r = v if r is None else r + v
-            for k in range(count):
-                total = total + jnp.where(
-                    apart == first + k - q, r[k * OWN : (k + 1) * OWN, :], 0.0
-                )
-    total = total * VOLUME
+    start = jnp.zeros((OWN, WIDE), jnp.float32)
+    total[...] = products(start, apart, bh, bl, 0, fh, fl, gh, gl, hh, hl)
+
+
+def band_kernel(
+    planes, xs, y_before, y_after, partial, own_start, wide_start, bh, bl, earlier,
+    band, image, fh, fl, gh, gl, hh, hl,
+):
+    outer_rows(xs, y_before, y_after, partial, image, fh, fl, gh, gl, hh, hl)
+    apart = difference(own_start, wide_start, planes)
+    total = products(earlier[...], apart, bh, bl, 1, fh, fl, gh, gl, hh, hl) * VOLUME
     for b in range(4):
         band[32 * b : 32 * b + 32, :] = total[32 * b : 32 * b + 32, 32 * b + 16 : 32 * b + 144]
 
@@ -217,9 +240,21 @@
                 ]
 
 
+def snake(k):
+    return k if k // LINE % 2 == 0 else k // LINE * LINE + LINE - 1 - k % LINE
+
+
 def shifted(x, axis, step):
     n = lax.axis_size(axis)
-    return lax.ppermute(x, axis, [(i, (i + step) % n) for i in range(n)])
+    at = snake if axis == "fn" else int
+    return lax.ppermute(x, axis, [(at(i), at((i + step) % n)) for i in range(n)])
+
+
+def exchanged(x):
+    order = [snake(k) for k in range(lax.axis_size("fn"))]
+    return lax.all_to_all(
+        x, "fn", split_axis=0, concat_axis=0, axis_index_groups=[order], tiled=True
+    )
 
 
 def body(coeffs, offsets, potential):
@@ -227,7 +262,10 @@
     position = lax.axis_index("fn")
     planes = potential.shape[0]
     padded = jnp.concatenate([offsets[-HALF:], offsets, offsets[:HALF]])
-    wide_start = lax.dynamic_slice(padded, (position * OWN,), (WIDE,))
+    line, along = position // LINE, position % LINE
+    number = jnp.where(line % 2 == 0, position, line * LINE + LINE - 1 - along)
+    wide_start = lax.dynamic_slice(padded, (number * OWN,), (WIDE,)).reshape(-1, 2, LINE)
+    wide_start = jnp.stack([wide_start[:, 0], wide_start[:, 1, ::-1]], axis=1).reshape(WIDE)
     own_start = wide_start[HALF : HALF + OWN]
     f32, bf16 = jnp.float32, jnp.bfloat16
     sds = jax.ShapeDtypeStruct
@@ -237,7 +275,7 @@
 
     pot = pl.pallas_call(
         potential_kernel,
-        out_shape=sds((OWN * PB, ROWS, CZ), f32),
+        out_shape=sds((OWN * BOX, CZ), f32),
         in_specs=[
             pl.BlockSpec(memory_space=pltpu.SMEM),
             pl.BlockSpec(memory_space=pltpu.VMEM),
@@ -246,13 +284,10 @@
         cost_estimate=cost(0, 4 << 20),
         name="box_potential",
     )(own_start, potential)
-    pot = pot.reshape(OWN * BOX, CZ)
     wide_start = wide_start[None, :]
     own_start = own_start[:, None]
 
-    x = lax.all_to_all(
-        coeffs.reshape(peers, 2 * BOX, CZ), "fn", split_axis=0, concat_axis=0, tiled=True
-    )
+    x = exchanged(coeffs.reshape(peers, 2 * BOX, CZ))
     x, pot, own_start, wide_start = lax.optimization_barrier((x, pot, own_start, wide_start))
     x = x.reshape(OWN * BOX, CZ)
     edge, halo = sds((OWN * PB, CZ), f32), sds((HALO * BOX, CZ), f32)
@@ -270,29 +305,35 @@
 
     image = sds((PB * 2 * OWN, CZ), f32)
     left = [sds((n * OWN, 2 * CZ), bf16) for n in (6, 6, 3, 3, 3, 3)]
-    own_bh, own_bl, image_in, partial, *ready = pl.pallas_call(
+    own = sds((PB, OWN, CELLS), bf16)
+    own_bh, own_bl, xs, image_in, partial, *inner = pl.pallas_call(
         inner_kernel,
-        out_shape=(sds((PB, OWN, CELLS), bf16), sds((PB, OWN, CELLS), bf16), image, image, *left),
+        out_shape=(own, own, sds((OWN * BOX, CZ), f32), image, image, *left),
         in_specs=[pl.BlockSpec(memory_space=pltpu.VMEM), pl.BlockSpec(memory_space=pl.ANY)],
         scratch_shapes=[pltpu.VMEM((OWN * BOX, CZ), f32), pltpu.SemaphoreType.DMA],
         compiler_params=vmem(20),
         cost_estimate=cost(1 << 30, 5 << 20),
         name="inner_rows",
     )(x, pot)
-
-    band, image_out, bh, bl = pl.pallas_call(
-        lambda *refs: band_kernel(planes, *refs),
+    bh, bl, inner_total = pl.pallas_call(
+        lambda *refs: inner_band_kernel(planes, *refs),
         out_shape=(
-            sds((OWN, CZ), f32),
-            image,
             sds((PB, WIDE, CELLS), bf16),
             sds((PB, WIDE, CELLS), bf16),
+            sds((OWN, WIDE), f32),
         ),
+        compiler_params=vmem(20),
+        cost_estimate=cost(1 << 30, 6 << 20),
+        name="inner_band",
+    )(low, high, own_start, wide_start, own_bh, own_bl, *inner)
+    band, image_out = pl.pallas_call(
+        lambda *refs: band_kernel(planes, *refs),
+        out_shape=(sds((OWN, CZ), f32), image),
         scratch_shapes=[pltpu.VMEM(v.shape, v.dtype) for v in left],
         compiler_params=vmem(20),
-        cost_estimate=cost(3 << 30, 8 << 20),
+        cost_estimate=cost(1 << 30, 6 << 20),
         name="band",
-    )(x, low, high, y_before, y_after, partial, own_start, wide_start, own_bh, own_bl, *ready)
+    )(xs, y_before, y_after, partial, own_start, wide_start, bh, bl, inner_total)
 
     bands = [band] + [shifted(band, "sub", k) for k in (1, 2, 3)]
     gradient = pl.pallas_call(
@@ -310,9 +351,7 @@
         *bands, image_in, image_out, bh.reshape(PB * WIDE, CELLS), bl.reshape(PB * WIDE, CELLS),
         own_start, wide_start,
     )
-    back = lax.all_to_all(
-        gradient.reshape(peers, 2, PB, ROWS, CZ), "fn", split_axis=0, concat_axis=0, tiled=True
-    )
+    back = exchanged(gradient.reshape(peers, 2, PB, ROWS, CZ))
     return back.reshape(coeffs.shape)
 
 

time: 105 us -> 103 us (0.981)
  blocking collectives: 38.1 us -> 35.6 us
  Pallas kernels: 11.5 us -> 9.92 us
  waiting for transfers between devices: 29.4 us -> 30.8 us
    all_to_all x1, blocking collectives: 38.1 us -> 35.6 us  [exchanged(): lax.all_to_all(x, 'fn', split_axis=0, concat_axis=0, axis_index_groups=[o...]
    ppermute x7, waiting for transfers between devices: 4.29 us -> 6 us  [shifted(): lax.ppermute(x, axis, [(at(i), at((i + step) % n)) for i in range(n)])]
    pallas_call x1, Pallas kernels: 3.1 us -> 1.51 us  [body(): pl.pallas_call(lambda *refs: band_kernel(planes, *refs), out_shape=(sds((...]
    pallas_call x2 -> x3, Pallas kernels: 5.02 us -> 4.82 us  [the longest x1 1.68 us: body(): pl.pallas_call(inner_kernel, out_shape=(own, own, sds((OWN * BOX, CZ), f3...]
  transfers between devices with their start and end apart: 8 -> 8, of which waited for: 4 -> 5; matrix products, arithmetic and copies ran while one was open for 0% -> 1% of each run, Pallas kernels for 5% -> 5%
where the time goes in v3:
time: 103 us; the launch traced here: 102 us
  blocking collectives  35.6 us (35%)
  waiting for transfers between devices  30.8 us (30%)
  starting transfers between devices  21.9 us (21%)
  Pallas kernels  9.92 us (10%)
  local copies, waits for them, and re-layouts  4.01 us (4%)
    all_to_all x1, blocking collectives, exchanged(): lax.all_to_all(x, 'fn', split_axis=0, concat_axis=0, axis_index_groups=[o...  35.6 us
    all_to_all x1, waiting for transfers between devices, exchanged(): lax.all_to_all(x, 'fn', split_axis=0, concat_axis=0, axis_index_groups=[o...  24.8 us
    all_to_all x1, starting transfers between devices, exchanged(): lax.all_to_all(x, 'fn', split_axis=0, concat_axis=0, axis_index_groups=[o...  13.1 us
    ppermute x7, starting transfers between devices, shifted(): lax.ppermute(x, axis, [(at(i), at((i + step) % n)) for i in range(n)])  8.77 us
    ppermute x7, waiting for transfers between devices, shifted(): lax.ppermute(x, axis, [(at(i), at((i + step) % n)) for i in range(n)])  6 us
    unnamed x9, local copies, waits for them, and re-layouts  3.16 us
    pallas_call x1, Pallas kernels, body(): pl.pallas_call(lambda *refs: update_kernel(planes, *refs), out_shape=sds(...  2.51 us
  transfers between devices with their start and end apart: 8, of which 5 were waited for; matrix products, arithmetic and copies ran while one was open for 1% of the time, Pallas kernels for 5%

profile of v3, /device:TPU:1, one launch (start us, length us, event | category | flops | bytes accessed | tf_op | source)
XLA Modules:
  0.0 102.4 jit_solution(12428124533568794317)
XLA Ops:
  0.0 13.1 %all-to-all-start = ((f32[64,32,128]{2,1,0:T(8,128)}), f32[64,32,128]{2,1,0:T(8,128)S(1)}, u32[]{:S(2)}, u32[]{:S(2)}) async-start(f32[64,32,128]{2,1,0:T(8,128)} %bitcast.12), calls=%async_computation | async-start | bytes 2097152 | tf_op jit(solution)/shard_map/all_to_all | solution.py:255
  13.2 0.1 fusion.1
  13.3 0.1 concatenate.3
  13.3 0.1 dynamic_slice.3
  13.4 0.1 reshape.25
  13.6 0.1 rev.3
  13.7 0.1 broadcast_in_dim.3
  13.8 0.1 slice.23.starts
  13.9 0.1 broadcast_in_dim_reshape.3.refs_3_.refs_5_.refs_9_
  14.0 1.6 %box_potential.1.pot_any = f32[2048,128]{1,0:T(8,128)S(1)} custom-call(s32[128]{0:T(128)S(1)} %slice.23.starts, f32[1024,4,128]{2,1,0:T(4,128)S(1)} %copy-done), custom_call_target="tpu_custom_call" | custom-call | bytes 4194304 | tf_op jit(solution)/shard_map/box_potential/pallas_call | solution.py:276
  15.6 0.0 copy-start.1
  15.6 1.0 copy-done.1
  16.6 24.8 %all-to-all-done = f32[64,32,128]{2,1,0:T(8,128)S(1)} async-done(((f32[64,32,128]{2,1,0:T(8,128)}), f32[64,32,128]{2,1,0:T(8,128)S(1)}, u32[]{:S(2)}, u32[]{:S(2)}) %all-to-all-start) | async-done | bytes 1048608 | tf_op jit(solution)/shard_map/all_to_all | solution.py:255
  41.4 1.1 %edges.1 = (f32[512,128]{1,0:T(8,128)S(1)}, f32[512,128]{1,0:T(8,128)}, f32[768,128]{1,0:T(8,128)S(1)}, f32[768,128]{1,0:T(8,128)S(1)}) custom-call(f32[2048,128]{1,0:T(8,128)S(1)} %bitcast.6), custom_call_target="tpu_custom_call" | custom-call | bytes 2097152 | tf_op jit(solution)/shard_map/edges/pallas_call | solution.py:294
  42.4 2.2 %collective-permute-start.2 = (f32[768,128]{1,0:T(8,128)S(1)}, f32[768,128]{1,0:T(8,128)S(1)}, u32[]{:S(2)}, u32[]{:S(2)}) collective-permute-start(f32[768,128]{1,0:T(8,128)S(1)} %get-tuple-element.37), channel_id=1, source_target_pairs={{0,4},{4,8},{8,12},{12,16},{16,20},{20,24},{24,28},{28,60},{60,56}... | collective-permute-start | bytes 1179656 | tf_op jit(solution)/shard_map/ppermute | solution.py:250
  44.6 1.3 %collective-permute-start = (f32[512,128]{1,0:T(8,128)}, f32[512,128]{1,0:T(8,128)S(1)}, u32[]{:S(2)}, u32[]{:S(2)}) collective-permute-start(f32[512,128]{1,0:T(8,128)} %get-tuple-element.32), channel_id=1, source_target_pairs={{0,1},{1,2},{2,3},{3,0},{4,5},{5,6},{6,7},{7,4},{8,9},{9,10},{10,1... | collective-permute-start | bytes 786440 | tf_op jit(solution)/shard_map/ppermute | solution.py:250
  45.9 1.4 %collective-permute-start.1 = (f32[512,128]{1,0:T(8,128)S(1)}, f32[512,128]{1,0:T(8,128)S(1)}, u32[]{:S(2)}, u32[]{:S(2)}) collective-permute-start(f32[512,128]{1,0:T(8,128)S(1)} %get-tuple-element.33), channel_id=1, source_target_pairs={{0,3},{1,0},{2,1},{3,2},{4,7},{5,4},{6,5},{7,6},{8,11},{9,8},{10,9... | collective-permute-start | bytes 786440 | tf_op jit(solution)/shard_map/ppermute | solution.py:250
  47.4 0.1 copy.8.refs_2_.refs_4_.refs_8_
  47.5 1.2 %copy-done.2 = f32[2048,128]{1,0:T(8,128)S(1)} copy-done((f32[2048,128]{1,0:T(8,128)S(1)}, f32[2048,128]{1,0:T(8,128)}, u32[]{:S(2)}) %copy-start.2) | copy-done | bytes 1048600
  48.7 1.7 %inner_rows.1 = (bf16[4,128,512]{2,1,0:T(8,128)(2,1)S(1)}, bf16[4,128,512]{2,1,0:T(8,128)(2,1)S(1)}, f32[2048,128]{1,0:T(8,128)S(1)}, f32[1024,128]{1,0:T(8,128)...) custom-call(f32[2048,128]{1,0:T(8,128)S(1)} %bitcast.7, ...), custom_call_target="tpu_custom_call" | custom-call | flops 1073741824 | bytes 5242880 | tf_op jit(solution)/shard_map/inner_rows/pallas_call | solution.py:309
  50.4 1.7 %collective-permute-done.3.refs_1_ = f32[768,128]{1,0:T(8,128)S(1)} collective-permute-done((f32[768,128]{1,0:T(8,128)S(1)}, f32[768,128]{1,0:T(8,128)S(1)}, u32[]{:S(2)}, u32[]{:S(2)}) %collective-permute-start.3) | collective-permute-done | bytes 393248 | tf_op jit(solution)/shard_map/ppermute | solution.py:250
  52.1 1.5 %inner_band.1 = (bf16[4,256,512]{2,1,0:T(8,128)(2,1)S(1)}, bf16[4,256,512]{2,1,0:T(8,128)(2,1)S(1)}, f32[128,256]{1,0:T(8,128)S(1)}) custom-call(f32[768,128]{1,0:T(8,128)S(1)} %collective-permute-done.2.refs_0_, f32[768,128]{1,0:T(8,128)S(1)} %collective-permute-done.3.refs_1_, s32[128,1]{1,0:T(8,128)S(1)} %copy.8.refs_2_.refs_4_.refs_8_, ...), custom_call_target="tpu_custom_call" | custom-call | flops 1073741824 | bytes 6291456 | tf_op jit(solution)/shard_map/inner_band/pallas_call | solution.py:318
  53.7 1.5 %band.1 = (f32[128,128]{1,0:T(8,128)S(1)}, f32[1024,128]{1,0:T(8,128)S(1)}) custom-call(f32[2048,128]{1,0:T(8,128)S(1)} %get-tuple-element.31.refs_0_, f32[512,128]{1,0:T(8,128)S(1)} %collective-permute-done.refs_1_, f32[512,128]{1,0:T(8,128)S(1)} %collective-permute-done.1.refs_2_, f32[1024,128]{1,0:T(8,128)S(1)} %get-tuple-element.34.refs_3_, ...), custom_call_target="tpu_custom_call" | custom-call | flops 1073741824 | bytes 6291456 | tf_op jit(solution)/shard_map/band/pallas_call | solution.py:329
  55.2 2.8 %collective-permute-start.6 = (f32[128,128]{1,0:T(8,128)S(1)}, f32[128,128]{1,0:T(8,128)S(1)}, u32[]{:S(2)}, u32[]{:S(2)}) collective-permute-start(f32[128,128]{1,0:T(8,128)S(1)} %get-tuple-element.50.refs_0_), channel_id=1, source_target_pairs={{0,3},{1,0},{2,1},{3,2},{4,7},{5,4},{6,5},{7,6},{8,11},{9,8},{10,9... | collective-permute-start | bytes 196616 | tf_op jit(solution)/shard_map/ppermute | solution.py:250
  58.0 0.4 collective-permute-start.5
  58.4 0.7 collective-permute-start.4
  59.1 0.3 collective-permute-done.6.refs_3_
  59.4 3.4 %collective-permute-done.5.refs_2_ = f32[128,128]{1,0:T(8,128)S(1)} collective-permute-done((f32[128,128]{1,0:T(8,128)S(1)}, f32[128,128]{1,0:T(8,128)S(1)}, u32[]{:S(2)}, u32[]{:S(2)}) %collective-permute-start.5) | collective-permute-done | bytes 65568 | tf_op jit(solution)/shard_map/ppermute | solution.py:250
  62.7 0.6 collective-permute-done.4.refs_1_
  63.3 2.5 %gradient.1 = f32[2048,128]{1,0:T(8,128)S(1)} custom-call(f32[128,128]{1,0:T(8,128)S(1)} %get-tuple-element.50.refs_0_, f32[128,128]{1,0:T(8,128)S(1)} %collective-permute-done.4.refs_1_, f32[128,128]{1,0:T(8,128)S(1)} %collective-permute-done.5.refs_2_, f32[128,128]{1,0:T(8,128)S(1)} %collective-permute-done.6.refs_3_, ...), custom_call_target="tpu_custom_call" | custom-call | flops 2147483648 | bytes 5242880 | tf_op jit(solution)/shard_map/gradient/pallas_call | solution.py:339
  65.9 35.6 %all_to_all.10 = f32[64,2,4,4,128]{4,3,2,1,0:T(4,128)S(1)} all-to-all(f32[64,2,4,4,128]{4,3,2,1,0:T(4,128)S(1)} %bitcast.10), channel_id=1, replica_groups={{0,4,8,12,16,20,24,28,60,56,52,48,44,40,36,32,64,68,72,76,80,84,88,92,1..., dimensions={0} | all-to-all | bytes 2097152 | tf_op jit(solution)/shard_map/all_to_all | solution.py:255
  101.5 1.0 copy.11
  (12 shorter events, 0.1 us)
Async XLA Ops:
  0.0 13.2 %copy-start.3 = (s32[8192]{0:T(1024)S(1)}, s32[8192]{0:T(1024)}, u32[]{:S(2)}) copy-start(s32[8192]{0:T(1024)} %param.4) | copy-start | bytes 98308
  0.0 14.0 %copy-start = (f32[1024,4,128]{2,1,0:T(4,128)S(1)}, f32[1024,4,128]{2,1,0:T(4,128)}, u32[]{:S(2)}) copy-start(f32[1024,4,128]{2,1,0:T(4,128)} %potential.1) | copy-start | bytes 6291460
  0.0 41.4 %all-to-all-start = ((f32[64,32,128]{2,1,0:T(8,128)}), f32[64,32,128]{2,1,0:T(8,128)S(1)}, u32[]{:S(2)}, u32[]{:S(2)}) async-start(f32[64,32,128]{2,1,0:T(8,128)} %bitcast.12), calls=%async_computation | async-start | bytes 2097152 | tf_op jit(solution)/shard_map/all_to_all | solution.py:255
  15.6 1.0 copy-start.1
  42.4 8.0 %collective-permute-start.2 = (f32[768,128]{1,0:T(8,128)S(1)}, f32[768,128]{1,0:T(8,128)S(1)}, u32[]{:S(2)}, u32[]{:S(2)}) collective-permute-start(f32[768,128]{1,0:T(8,128)S(1)} %get-tuple-element.37), channel_id=1, source_target_pairs={{0,4},{4,8},{8,12},{12,16},{16,20},{20,24},{24,28},{28,60},{60,56}... | collective-permute-start | bytes 1179656 | tf_op jit(solution)/shard_map/ppermute | solution.py:250
  44.6 7.5 %collective-permute-start.3 = (f32[768,128]{1,0:T(8,128)S(1)}, f32[768,128]{1,0:T(8,128)S(1)}, u32[]{:S(2)}, u32[]{:S(2)}) collective-permute-start(f32[768,128]{1,0:T(8,128)S(1)} %get-tuple-element.38), channel_id=1, source_target_pairs={{0,224},{4,0},{8,4},{12,8},{16,12},{20,16},{24,20},{28,24},{60,28}... | collective-permute-start | bytes 1179656 | tf_op jit(solution)/shard_map/ppermute | solution.py:250
  44.6 9.0 %collective-permute-start = (f32[512,128]{1,0:T(8,128)}, f32[512,128]{1,0:T(8,128)S(1)}, u32[]{:S(2)}, u32[]{:S(2)}) collective-permute-start(f32[512,128]{1,0:T(8,128)} %get-tuple-element.32), channel_id=1, source_target_pairs={{0,1},{1,2},{2,3},{3,0},{4,5},{5,6},{6,7},{7,4},{8,9},{9,10},{10,1... | collective-permute-start | bytes 786440 | tf_op jit(solution)/shard_map/ppermute | solution.py:250
  45.9 7.8 %collective-permute-start.1 = (f32[512,128]{1,0:T(8,128)S(1)}, f32[512,128]{1,0:T(8,128)S(1)}, u32[]{:S(2)}, u32[]{:S(2)}) collective-permute-start(f32[512,128]{1,0:T(8,128)S(1)} %get-tuple-element.33), channel_id=1, source_target_pairs={{0,3},{1,0},{2,1},{3,2},{4,7},{5,4},{6,5},{7,6},{8,11},{9,8},{10,9... | collective-permute-start | bytes 786440 | tf_op jit(solution)/shard_map/ppermute | solution.py:250
  47.5 1.2 %copy-start.2 = (f32[2048,128]{1,0:T(8,128)S(1)}, f32[2048,128]{1,0:T(8,128)}, u32[]{:S(2)}) copy-start(f32[2048,128]{1,0:T(8,128)} %copy-done.1) | copy-start | bytes 3145732
  55.2 4.1 %collective-permute-start.6 = (f32[128,128]{1,0:T(8,128)S(1)}, f32[128,128]{1,0:T(8,128)S(1)}, u32[]{:S(2)}, u32[]{:S(2)}) collective-permute-start(f32[128,128]{1,0:T(8,128)S(1)} %get-tuple-element.50.refs_0_), channel_id=1, source_target_pairs={{0,3},{1,0},{2,1},{3,2},{4,7},{5,4},{6,5},{7,6},{8,11},{9,8},{10,9... | collective-permute-start | bytes 196616 | tf_op jit(solution)/shard_map/ppermute | solution.py:250
  58.0 4.7 %collective-permute-start.5 = (f32[128,128]{1,0:T(8,128)S(1)}, f32[128,128]{1,0:T(8,128)S(1)}, u32[]{:S(2)}, u32[]{:S(2)}) collective-permute-start(f32[128,128]{1,0:T(8,128)S(1)} %get-tuple-element.50.refs_0_), channel_id=1, source_target_pairs={{0,2},{1,3},{2,0},{3,1},{4,6},{5,7},{6,4},{7,5},{8,10},{9,11},{10,... | collective-permute-start | bytes 196616 | tf_op jit(solution)/shard_map/ppermute | solution.py:250
  58.4 5.0 %collective-permute-start.4 = (f32[128,128]{1,0:T(8,128)S(1)}, f32[128,128]{1,0:T(8,128)S(1)}, u32[]{:S(2)}, u32[]{:S(2)}) collective-permute-start(f32[128,128]{1,0:T(8,128)S(1)} %get-tuple-element.50.refs_0_), channel_id=1, source_target_pairs={{0,1},{1,2},{2,3},{3,0},{4,5},{5,6},{6,7},{7,4},{8,9},{9,10},{10,1... | collective-permute-start | bytes 196616 | tf_op jit(solution)/shard_map/ppermute | solution.py:250

commit v4 on v3

--- a/solution.py
+++ b/solution.py
@@ -207,7 +207,7 @@
 
 
 def update_kernel(
-    planes, b0, b1, b2, b3, image_in, image_out, bh, bl, own_start, wide_start, out, wh, wl, wide
+    planes, b0, b1, b2, b3, image_in, image_out, bh, bl, own_start, wide_start, out, w, wide
 ):
     band = b0[...] + b1[...] + b2[...] + b3[...]
     for b in range(4):
@@ -222,12 +222,14 @@
         for p in range(PB):
             q = p - d
             if 0 <= q < PB:
-                wh[p * OWN : (p + 1) * OWN, q * WIDE : (q + 1) * WIDE] = hi
-                wl[p * OWN : (p + 1) * OWN, q * WIDE : (q + 1) * WIDE] = lo
+                cols = slice(q * WIDE, (q + 1) * WIDE)
+                w[p * OWN : (p + 1) * OWN, cols] = hi
+                w[(PB + p) * OWN : (PB + p + 1) * OWN, cols] = lo
     def dot(a, b):
         return jnp.dot(a, b, preferred_element_type=jnp.float32)
 
-    r = dot(wh[...], bh[...]) + dot(wh[...], bl[...]) + dot(wl[...], bh[...])
+    both = dot(w[...], bh[...])
+    r = both[: PB * OWN, :] + both[PB * OWN :, :] + dot(w[: PB * OWN, :], bl[...])
     for p in range(PB):
         for at, y in enumerate(ORDER):
             image = (image_in, image_out)[at // 2]
@@ -335,13 +337,12 @@
         name="band",
     )(xs, y_before, y_after, partial, own_start, wide_start, bh, bl, inner_total)
 
-    bands = [band] + [shifted(band, "sub", k) for k in (1, 2, 3)]
+    bands = [band] + [shifted(band, "sub", k) for k in (3, 2, 1)]
     gradient = pl.pallas_call(
         lambda *refs: update_kernel(planes, *refs),
         out_shape=sds((OWN * BOX, CZ), f32),
         scratch_shapes=[
-            pltpu.VMEM((PB * OWN, PB * WIDE), bf16),
-            pltpu.VMEM((PB * OWN, PB * WIDE), bf16),
+            pltpu.VMEM((2 * PB * OWN, PB * WIDE), bf16),
             pltpu.VMEM((OWN, WIDE), f32),
         ],
         compiler_params=vmem(20),

time: 103 us -> 102 us (level)
  waiting for transfers between devices: 30.8 us -> 29.3 us
  starting transfers between devices: 21.9 us -> 23.1 us
    ppermute x7, waiting for transfers between devices: 6 us -> 4.53 us  [shifted(): lax.ppermute(x, axis, [(at(i), at((i + step) % n)) for i in range(n)])]
    ppermute x7, starting transfers between devices: 8.77 us -> 9.99 us  [shifted(): lax.ppermute(x, axis, [(at(i), at((i + step) % n)) for i in range(n)])]
  transfers between devices with their start and end apart: 8 -> 8, of which waited for: 5 -> 4; matrix products, arithmetic and copies ran while one was open for 1% -> 1% of each run, Pallas kernels for 5% -> 5%
where the time goes in v4:
time: 102 us
  blocking collectives  35.1 us (34%)
  waiting for transfers between devices  29.3 us (29%)
  starting transfers between devices  23.1 us (23%)
  Pallas kernels  9.95 us (10%)
  local copies, waits for them, and re-layouts  4.01 us (4%)
    all_to_all x1, blocking collectives, exchanged(): lax.all_to_all(x, 'fn', split_axis=0, concat_axis=0, axis_index_groups=[o...  35.1 us
    all_to_all x1, waiting for transfers between devices, exchanged(): lax.all_to_all(x, 'fn', split_axis=0, concat_axis=0, axis_index_groups=[o...  24.8 us
    all_to_all x1, starting transfers between devices, exchanged(): lax.all_to_all(x, 'fn', split_axis=0, concat_axis=0, axis_index_groups=[o...  13.1 us
    ppermute x7, starting transfers between devices, shifted(): lax.ppermute(x, axis, [(at(i), at((i + step) % n)) for i in range(n)])  9.99 us
    ppermute x7, waiting for transfers between devices, shifted(): lax.ppermute(x, axis, [(at(i), at((i + step) % n)) for i in range(n)])  4.53 us
    unnamed x9, local copies, waits for them, and re-layouts  3.16 us
    pallas_call x1, Pallas kernels, body(): pl.pallas_call(lambda *refs: update_kernel(planes, *refs), out_shape=sds(...  2.53 us
  transfers between devices with their start and end apart: 8, of which 4 were waited for; matrix products, arithmetic and copies ran while one was open for 1% of the time, Pallas kernels for 5%

profile of v4, /device:TPU:1, one launch (start us, length us, event | category | flops | bytes accessed | tf_op | source)
XLA Modules:
  0.0 101.7 jit_solution(4873707910681505419)
XLA Ops:
  0.0 13.1 %all-to-all-start = ((f32[64,32,128]{2,1,0:T(8,128)}), f32[64,32,128]{2,1,0:T(8,128)S(1)}, u32[]{:S(2)}, u32[]{:S(2)}) async-start(f32[64,32,128]{2,1,0:T(8,128)} %bitcast.12), calls=%async_computation | async-start | bytes 2097152 | tf_op jit(solution)/shard_map/all_to_all | solution.py:257
  13.2 0.1 fusion.1
  13.3 0.1 concatenate.3
  13.3 0.1 dynamic_slice.3
  13.4 0.1 reshape.25
  13.6 0.1 rev.3
  13.7 0.1 broadcast_in_dim.3
  13.8 0.1 slice.23.starts
  13.9 0.1 broadcast_in_dim_reshape.3.refs_3_.refs_5_.refs_9_
  14.0 1.6 %box_potential.1.pot_any = f32[2048,128]{1,0:T(8,128)S(1)} custom-call(s32[128]{0:T(128)S(1)} %slice.23.starts, f32[1024,4,128]{2,1,0:T(4,128)S(1)} %copy-done), custom_call_target="tpu_custom_call" | custom-call | bytes 4194304 | tf_op jit(solution)/shard_map/box_potential/pallas_call | solution.py:278
  15.6 0.0 copy-start.1
  15.6 1.0 copy-done.1
  16.6 24.8 %all-to-all-done = f32[64,32,128]{2,1,0:T(8,128)S(1)} async-done(((f32[64,32,128]{2,1,0:T(8,128)}), f32[64,32,128]{2,1,0:T(8,128)S(1)}, u32[]{:S(2)}, u32[]{:S(2)}) %all-to-all-start) | async-done | bytes 1048608 | tf_op jit(solution)/shard_map/all_to_all | solution.py:257
  41.4 1.1 %edges.1 = (f32[512,128]{1,0:T(8,128)S(1)}, f32[512,128]{1,0:T(8,128)}, f32[768,128]{1,0:T(8,128)S(1)}, f32[768,128]{1,0:T(8,128)S(1)}) custom-call(f32[2048,128]{1,0:T(8,128)S(1)} %bitcast.6), custom_call_target="tpu_custom_call" | custom-call | bytes 2097152 | tf_op jit(solution)/shard_map/edges/pallas_call | solution.py:296
  42.4 2.2 %collective-permute-start.2 = (f32[768,128]{1,0:T(8,128)S(1)}, f32[768,128]{1,0:T(8,128)S(1)}, u32[]{:S(2)}, u32[]{:S(2)}) collective-permute-start(f32[768,128]{1,0:T(8,128)S(1)} %get-tuple-element.37), channel_id=1, source_target_pairs={{0,4},{4,8},{8,12},{12,16},{16,20},{20,24},{24,28},{28,60},{60,56}... | collective-permute-start | bytes 1179656 | tf_op jit(solution)/shard_map/ppermute | solution.py:252
  44.6 0.0 collective-permute-start.3
  44.6 1.3 %collective-permute-start = (f32[512,128]{1,0:T(8,128)}, f32[512,128]{1,0:T(8,128)S(1)}, u32[]{:S(2)}, u32[]{:S(2)}) collective-permute-start(f32[512,128]{1,0:T(8,128)} %get-tuple-element.32), channel_id=1, source_target_pairs={{0,1},{1,2},{2,3},{3,0},{4,5},{5,6},{6,7},{7,4},{8,9},{9,10},{10,1... | collective-permute-start | bytes 786440 | tf_op jit(solution)/shard_map/ppermute | solution.py:252
  45.9 1.4 %collective-permute-start.1 = (f32[512,128]{1,0:T(8,128)S(1)}, f32[512,128]{1,0:T(8,128)S(1)}, u32[]{:S(2)}, u32[]{:S(2)}) collective-permute-start(f32[512,128]{1,0:T(8,128)S(1)} %get-tuple-element.33), channel_id=1, source_target_pairs={{0,3},{1,0},{2,1},{3,2},{4,7},{5,4},{6,5},{7,6},{8,11},{9,8},{10,9... | collective-permute-start | bytes 786440 | tf_op jit(solution)/shard_map/ppermute | solution.py:252
  47.4 0.1 copy.8.refs_2_.refs_4_.refs_8_
  47.5 1.2 %copy-done.2 = f32[2048,128]{1,0:T(8,128)S(1)} copy-done((f32[2048,128]{1,0:T(8,128)S(1)}, f32[2048,128]{1,0:T(8,128)}, u32[]{:S(2)}) %copy-start.2) | copy-done | bytes 1048600
  48.7 1.7 %inner_rows.1 = (bf16[4,128,512]{2,1,0:T(8,128)(2,1)S(1)}, bf16[4,128,512]{2,1,0:T(8,128)(2,1)S(1)}, f32[2048,128]{1,0:T(8,128)S(1)}, f32[1024,128]{1,0:T(8,128)...) custom-call(f32[2048,128]{1,0:T(8,128)S(1)} %bitcast.7, ...), custom_call_target="tpu_custom_call" | custom-call | flops 1073741824 | bytes 5242880 | tf_op jit(solution)/shard_map/inner_rows/pallas_call | solution.py:311
  50.4 1.7 %collective-permute-done.3.refs_1_ = f32[768,128]{1,0:T(8,128)S(1)} collective-permute-done((f32[768,128]{1,0:T(8,128)S(1)}, f32[768,128]{1,0:T(8,128)S(1)}, u32[]{:S(2)}, u32[]{:S(2)}) %collective-permute-start.3) | collective-permute-done | bytes 393248 | tf_op jit(solution)/shard_map/ppermute | solution.py:252
  52.1 1.5 %inner_band.1 = (bf16[4,256,512]{2,1,0:T(8,128)(2,1)S(1)}, bf16[4,256,512]{2,1,0:T(8,128)(2,1)S(1)}, f32[128,256]{1,0:T(8,128)S(1)}) custom-call(f32[768,128]{1,0:T(8,128)S(1)} %collective-permute-done.2.refs_0_, f32[768,128]{1,0:T(8,128)S(1)} %collective-permute-done.3.refs_1_, s32[128,1]{1,0:T(8,128)S(1)} %copy.8.refs_2_.refs_4_.refs_8_, ...), custom_call_target="tpu_custom_call" | custom-call | flops 1073741824 | bytes 6291456 | tf_op jit(solution)/shard_map/inner_band/pallas_call | solution.py:320
  53.7 1.5 %band.1 = (f32[128,128]{1,0:T(8,128)S(1)}, f32[1024,128]{1,0:T(8,128)S(1)}) custom-call(f32[2048,128]{1,0:T(8,128)S(1)} %get-tuple-element.31.refs_0_, f32[512,128]{1,0:T(8,128)S(1)} %collective-permute-done.refs_1_, f32[512,128]{1,0:T(8,128)S(1)} %collective-permute-done.1.refs_2_, f32[1024,128]{1,0:T(8,128)S(1)} %get-tuple-element.34.refs_3_, ...), custom_call_target="tpu_custom_call" | custom-call | flops 1073741824 | bytes 6291456 | tf_op jit(solution)/shard_map/band/pallas_call | solution.py:331
  55.2 1.4 %collective-permute-start.6 = (f32[128,128]{1,0:T(8,128)S(1)}, f32[128,128]{1,0:T(8,128)S(1)}, u32[]{:S(2)}, u32[]{:S(2)}) collective-permute-start(f32[128,128]{1,0:T(8,128)S(1)} %get-tuple-element.50.refs_0_), channel_id=1, source_target_pairs={{0,1},{1,2},{2,3},{3,0},{4,5},{5,6},{6,7},{7,4},{8,9},{9,10},{10,1... | collective-permute-start | bytes 196616 | tf_op jit(solution)/shard_map/ppermute | solution.py:252
  56.6 2.6 %collective-permute-start.5 = (f32[128,128]{1,0:T(8,128)S(1)}, f32[128,128]{1,0:T(8,128)S(1)}, u32[]{:S(2)}, u32[]{:S(2)}) collective-permute-start(f32[128,128]{1,0:T(8,128)S(1)} %get-tuple-element.50.refs_0_), channel_id=1, source_target_pairs={{0,2},{1,3},{2,0},{3,1},{4,6},{5,7},{6,4},{7,5},{8,10},{9,11},{10,... | collective-permute-start | bytes 196616 | tf_op jit(solution)/shard_map/ppermute | solution.py:252
  59.2 1.1 %collective-permute-start.4 = (f32[128,128]{1,0:T(8,128)S(1)}, f32[128,128]{1,0:T(8,128)S(1)}, u32[]{:S(2)}, u32[]{:S(2)}) collective-permute-start(f32[128,128]{1,0:T(8,128)S(1)} %get-tuple-element.50.refs_0_), channel_id=1, source_target_pairs={{0,3},{1,0},{2,1},{3,2},{4,7},{5,4},{6,5},{7,6},{8,11},{9,8},{10,9... | collective-permute-start | bytes 196616 | tf_op jit(solution)/shard_map/ppermute | solution.py:252
  60.3 1.4 %collective-permute-done.5.refs_2_ = f32[128,128]{1,0:T(8,128)S(1)} collective-permute-done((f32[128,128]{1,0:T(8,128)S(1)}, f32[128,128]{1,0:T(8,128)S(1)}, u32[]{:S(2)}, u32[]{:S(2)}) %collective-permute-start.5) | collective-permute-done | bytes 65568 | tf_op jit(solution)/shard_map/ppermute | solution.py:252
  61.7 1.4 %collective-permute-done.4.refs_1_ = f32[128,128]{1,0:T(8,128)S(1)} collective-permute-done((f32[128,128]{1,0:T(8,128)S(1)}, f32[128,128]{1,0:T(8,128)S(1)}, u32[]{:S(2)}, u32[]{:S(2)}) %collective-permute-start.4) | collective-permute-done | bytes 65568 | tf_op jit(solution)/shard_map/ppermute | solution.py:252
  63.1 2.5 %gradient.1 = f32[2048,128]{1,0:T(8,128)S(1)} custom-call(f32[128,128]{1,0:T(8,128)S(1)} %get-tuple-element.50.refs_0_, f32[128,128]{1,0:T(8,128)S(1)} %collective-permute-done.4.refs_1_, f32[128,128]{1,0:T(8,128)S(1)} %collective-permute-done.5.refs_2_, f32[128,128]{1,0:T(8,128)S(1)} %collective-permute-done.6.refs_3_, ...), custom_call_target="tpu_custom_call" | custom-call | flops 2147483648 | bytes 5242880 | tf_op jit(solution)/shard_map/gradient/pallas_call | solution.py:341
  65.6 35.1 %all_to_all.10 = f32[64,2,4,4,128]{4,3,2,1,0:T(4,128)S(1)} all-to-all(f32[64,2,4,4,128]{4,3,2,1,0:T(4,128)S(1)} %bitcast.10), channel_id=1, replica_groups={{0,4,8,12,16,20,24,28,60,56,52,48,44,40,36,32,64,68,72,76,80,84,88,92,1..., dimensions={0} | all-to-all | bytes 2097152 | tf_op jit(solution)/shard_map/all_to_all | solution.py:257
  100.7 1.0 copy.11
  (12 shorter events, 0.1 us)
Async XLA Ops:
  0.0 13.2 %copy-start.3 = (s32[8192]{0:T(1024)S(1)}, s32[8192]{0:T(1024)}, u32[]{:S(2)}) copy-start(s32[8192]{0:T(1024)} %param.4) | copy-start | bytes 98308
  0.0 14.0 %copy-start = (f32[1024,4,128]{2,1,0:T(4,128)S(1)}, f32[1024,4,128]{2,1,0:T(4,128)}, u32[]{:S(2)}) copy-start(f32[1024,4,128]{2,1,0:T(4,128)} %potential.1) | copy-start | bytes 6291460
  0.0 41.4 %all-to-all-start = ((f32[64,32,128]{2,1,0:T(8,128)}), f32[64,32,128]{2,1,0:T(8,128)S(1)}, u32[]{:S(2)}, u32[]{:S(2)}) async-start(f32[64,32,128]{2,1,0:T(8,128)} %bitcast.12), calls=%async_computation | async-start | bytes 2097152 | tf_op jit(solution)/shard_map/all_to_all | solution.py:257
  15.6 1.0 copy-start.1
  42.4 8.0 %collective-permute-start.2 = (f32[768,128]{1,0:T(8,128)S(1)}, f32[768,128]{1,0:T(8,128)S(1)}, u32[]{:S(2)}, u32[]{:S(2)}) collective-permute-start(f32[768,128]{1,0:T(8,128)S(1)} %get-tuple-element.37), channel_id=1, source_target_pairs={{0,4},{4,8},{8,12},{12,16},{16,20},{20,24},{24,28},{28,60},{60,56}... | collective-permute-start | bytes 1179656 | tf_op jit(solution)/shard_map/ppermute | solution.py:252
  44.6 7.5 %collective-permute-start.3 = (f32[768,128]{1,0:T(8,128)S(1)}, f32[768,128]{1,0:T(8,128)S(1)}, u32[]{:S(2)}, u32[]{:S(2)}) collective-permute-start(f32[768,128]{1,0:T(8,128)S(1)} %get-tuple-element.38), channel_id=1, source_target_pairs={{0,224},{4,0},{8,4},{12,8},{16,12},{20,16},{24,20},{28,24},{60,28}... | collective-permute-start | bytes 1179656 | tf_op jit(solution)/shard_map/ppermute | solution.py:252
  44.6 9.0 %collective-permute-start = (f32[512,128]{1,0:T(8,128)}, f32[512,128]{1,0:T(8,128)S(1)}, u32[]{:S(2)}, u32[]{:S(2)}) collective-permute-start(f32[512,128]{1,0:T(8,128)} %get-tuple-element.32), channel_id=1, source_target_pairs={{0,1},{1,2},{2,3},{3,0},{4,5},{5,6},{6,7},{7,4},{8,9},{9,10},{10,1... | collective-permute-start | bytes 786440 | tf_op jit(solution)/shard_map/ppermute | solution.py:252
  45.9 7.8 %collective-permute-start.1 = (f32[512,128]{1,0:T(8,128)S(1)}, f32[512,128]{1,0:T(8,128)S(1)}, u32[]{:S(2)}, u32[]{:S(2)}) collective-permute-start(f32[512,128]{1,0:T(8,128)S(1)} %get-tuple-element.33), channel_id=1, source_target_pairs={{0,3},{1,0},{2,1},{3,2},{4,7},{5,4},{6,5},{7,6},{8,11},{9,8},{10,9... | collective-permute-start | bytes 786440 | tf_op jit(solution)/shard_map/ppermute | solution.py:252
  47.5 1.2 %copy-start.2 = (f32[2048,128]{1,0:T(8,128)S(1)}, f32[2048,128]{1,0:T(8,128)}, u32[]{:S(2)}) copy-start(f32[2048,128]{1,0:T(8,128)} %copy-done.1) | copy-start | bytes 3145732
  55.2 5.1 %collective-permute-start.6 = (f32[128,128]{1,0:T(8,128)S(1)}, f32[128,128]{1,0:T(8,128)S(1)}, u32[]{:S(2)}, u32[]{:S(2)}) collective-permute-start(f32[128,128]{1,0:T(8,128)S(1)} %get-tuple-element.50.refs_0_), channel_id=1, source_target_pairs={{0,1},{1,2},{2,3},{3,0},{4,5},{5,6},{6,7},{7,4},{8,9},{9,10},{10,1... | collective-permute-start | bytes 196616 | tf_op jit(solution)/shard_map/ppermute | solution.py:252
  56.6 5.1 %collective-permute-start.5 = (f32[128,128]{1,0:T(8,128)S(1)}, f32[128,128]{1,0:T(8,128)S(1)}, u32[]{:S(2)}, u32[]{:S(2)}) collective-permute-start(f32[128,128]{1,0:T(8,128)S(1)} %get-tuple-element.50.refs_0_), channel_id=1, source_target_pairs={{0,2},{1,3},{2,0},{3,1},{4,6},{5,7},{6,4},{7,5},{8,10},{9,11},{10,... | collective-permute-start | bytes 196616 | tf_op jit(solution)/shard_map/ppermute | solution.py:252
  59.2 3.9 %collective-permute-start.4 = (f32[128,128]{1,0:T(8,128)S(1)}, f32[128,128]{1,0:T(8,128)S(1)}, u32[]{:S(2)}, u32[]{:S(2)}) collective-permute-start(f32[128,128]{1,0:T(8,128)S(1)} %get-tuple-element.50.refs_0_), channel_id=1, source_target_pairs={{0,3},{1,0},{2,1},{3,2},{4,7},{5,4},{6,5},{7,6},{8,11},{9,8},{10,9... | collective-permute-start | bytes 196616 | tf_op jit(solution)/shard_map/ppermute | solution.py:252

commit v5 on v4

--- a/solution.py
+++ b/solution.py
@@ -165,8 +165,8 @@
         right_hi, right_lo = bh[q, :, cols], bl[q, :, cols]
         for hi, lo, at, count, first in pieces[q]:
             rows = slice(at * OWN, (at + count) * OWN)
-            r = dot_t(hi[rows, :], right_hi) + dot_t(hi[rows, :], right_lo)
-            r = r + dot_t(lo[rows, :], right_hi)
+            both = dot_t(jnp.concatenate([hi[rows, :], lo[rows, :]], axis=0), right_hi)
+            r = both[: count * OWN, :] + both[count * OWN :, :] + dot_t(hi[rows, :], right_lo)
             for k in range(count):
                 total = total + jnp.where(
                     apart == first + k - q, r[k * OWN : (k + 1) * OWN, :], 0.0

time: 102 us -> 102 us (level)
  no operation moved by 1% of the time
where the time goes in v5:
time: 102 us
  blocking collectives  35.1 us (34%)
  waiting for transfers between devices  29.3 us (29%)
  starting transfers between devices  23.1 us (23%)
  Pallas kernels  9.95 us (10%)
  local copies, waits for them, and re-layouts  4.01 us (4%)
    all_to_all x1, blocking collectives, exchanged(): lax.all_to_all(x, 'fn', split_axis=0, concat_axis=0, axis_index_groups=[o...  35.1 us
    all_to_all x1, waiting for transfers between devices, exchanged(): lax.all_to_all(x, 'fn', split_axis=0, concat_axis=0, axis_index_groups=[o...  24.8 us
    all_to_all x1, starting transfers between devices, exchanged(): lax.all_to_all(x, 'fn', split_axis=0, concat_axis=0, axis_index_groups=[o...  13.1 us
    ppermute x7, starting transfers between devices, shifted(): lax.ppermute(x, axis, [(at(i), at((i + step) % n)) for i in range(n)])  10 us
    ppermute x7, waiting for transfers between devices, shifted(): lax.ppermute(x, axis, [(at(i), at((i + step) % n)) for i in range(n)])  4.52 us
    unnamed x9, local copies, waits for them, and re-layouts  3.16 us
    pallas_call x1, Pallas kernels, body(): pl.pallas_call(lambda *refs: update_kernel(planes, *refs), out_shape=sds(...  2.53 us
  transfers between devices with their start and end apart: 8, of which 4 were waited for; matrix products, arithmetic and copies ran while one was open for 1% of the time, Pallas kernels for 5%

profile of v5, /device:TPU:1, one launch (start us, length us, event | category | flops | bytes accessed | tf_op | source)
XLA Modules:
  0.0 101.7 jit_solution(15189196926525720029)
XLA Ops:
  0.0 13.1 %all-to-all-start = ((f32[64,32,128]{2,1,0:T(8,128)}), f32[64,32,128]{2,1,0:T(8,128)S(1)}, u32[]{:S(2)}, u32[]{:S(2)}) async-start(f32[64,32,128]{2,1,0:T(8,128)} %bitcast.12), calls=%async_computation | async-start | bytes 2097152 | tf_op jit(solution)/shard_map/all_to_all | solution.py:257
  13.2 0.1 fusion.1
  13.3 0.1 concatenate.3
  13.3 0.1 dynamic_slice.3
  13.4 0.1 reshape.25
  13.6 0.1 rev.3
  13.7 0.1 broadcast_in_dim.3
  13.8 0.1 slice.23.starts
  13.9 0.1 broadcast_in_dim_reshape.3.refs_3_.refs_5_.refs_9_
  14.0 1.6 %box_potential.1.pot_any = f32[2048,128]{1,0:T(8,128)S(1)} custom-call(s32[128]{0:T(128)S(1)} %slice.23.starts, f32[1024,4,128]{2,1,0:T(4,128)S(1)} %copy-done), custom_call_target="tpu_custom_call" | custom-call | bytes 4194304 | tf_op jit(solution)/shard_map/box_potential/pallas_call | solution.py:278
  15.6 0.0 copy-start.1
  15.6 1.0 copy-done.1
  16.6 24.8 %all-to-all-done = f32[64,32,128]{2,1,0:T(8,128)S(1)} async-done(((f32[64,32,128]{2,1,0:T(8,128)}), f32[64,32,128]{2,1,0:T(8,128)S(1)}, u32[]{:S(2)}, u32[]{:S(2)}) %all-to-all-start) | async-done | bytes 1048608 | tf_op jit(solution)/shard_map/all_to_all | solution.py:257
  41.4 1.1 %edges.1 = (f32[512,128]{1,0:T(8,128)S(1)}, f32[512,128]{1,0:T(8,128)}, f32[768,128]{1,0:T(8,128)S(1)}, f32[768,128]{1,0:T(8,128)S(1)}) custom-call(f32[2048,128]{1,0:T(8,128)S(1)} %bitcast.6), custom_call_target="tpu_custom_call" | custom-call | bytes 2097152 | tf_op jit(solution)/shard_map/edges/pallas_call | solution.py:296
  42.4 2.2 %collective-permute-start.2 = (f32[768,128]{1,0:T(8,128)S(1)}, f32[768,128]{1,0:T(8,128)S(1)}, u32[]{:S(2)}, u32[]{:S(2)}) collective-permute-start(f32[768,128]{1,0:T(8,128)S(1)} %get-tuple-element.37), channel_id=1, source_target_pairs={{0,4},{4,8},{8,12},{12,16},{16,20},{20,24},{24,28},{28,60},{60,56}... | collective-permute-start | bytes 1179656 | tf_op jit(solution)/shard_map/ppermute | solution.py:252
  44.6 1.3 %collective-permute-start = (f32[512,128]{1,0:T(8,128)}, f32[512,128]{1,0:T(8,128)S(1)}, u32[]{:S(2)}, u32[]{:S(2)}) collective-permute-start(f32[512,128]{1,0:T(8,128)} %get-tuple-element.32), channel_id=1, source_target_pairs={{0,1},{1,2},{2,3},{3,0},{4,5},{5,6},{6,7},{7,4},{8,9},{9,10},{10,1... | collective-permute-start | bytes 786440 | tf_op jit(solution)/shard_map/ppermute | solution.py:252
  45.9 1.4 %collective-permute-start.1 = (f32[512,128]{1,0:T(8,128)S(1)}, f32[512,128]{1,0:T(8,128)S(1)}, u32[]{:S(2)}, u32[]{:S(2)}) collective-permute-start(f32[512,128]{1,0:T(8,128)S(1)} %get-tuple-element.33), channel_id=1, source_target_pairs={{0,3},{1,0},{2,1},{3,2},{4,7},{5,4},{6,5},{7,6},{8,11},{9,8},{10,9... | collective-permute-start | bytes 786440 | tf_op jit(solution)/shard_map/ppermute | solution.py:252
  47.4 0.1 copy.8.refs_2_.refs_4_.refs_8_
  47.5 1.2 %copy-done.2 = f32[2048,128]{1,0:T(8,128)S(1)} copy-done((f32[2048,128]{1,0:T(8,128)S(1)}, f32[2048,128]{1,0:T(8,128)}, u32[]{:S(2)}) %copy-start.2) | copy-done | bytes 1048600
  48.7 1.7 %inner_rows.1 = (bf16[4,128,512]{2,1,0:T(8,128)(2,1)S(1)}, bf16[4,128,512]{2,1,0:T(8,128)(2,1)S(1)}, f32[2048,128]{1,0:T(8,128)S(1)}, f32[1024,128]{1,0:T(8,128)...) custom-call(f32[2048,128]{1,0:T(8,128)S(1)} %bitcast.7, ...), custom_call_target="tpu_custom_call" | custom-call | flops 1073741824 | bytes 5242880 | tf_op jit(solution)/shard_map/inner_rows/pallas_call | solution.py:311
  50.4 1.7 %collective-permute-done.3.refs_1_ = f32[768,128]{1,0:T(8,128)S(1)} collective-permute-done((f32[768,128]{1,0:T(8,128)S(1)}, f32[768,128]{1,0:T(8,128)S(1)}, u32[]{:S(2)}, u32[]{:S(2)}) %collective-permute-start.3) | collective-permute-done | bytes 393248 | tf_op jit(solution)/shard_map/ppermute | solution.py:252
  52.1 1.5 %inner_band.1 = (bf16[4,256,512]{2,1,0:T(8,128)(2,1)S(1)}, bf16[4,256,512]{2,1,0:T(8,128)(2,1)S(1)}, f32[128,256]{1,0:T(8,128)S(1)}) custom-call(f32[768,128]{1,0:T(8,128)S(1)} %collective-permute-done.2.refs_0_, f32[768,128]{1,0:T(8,128)S(1)} %collective-permute-done.3.refs_1_, s32[128,1]{1,0:T(8,128)S(1)} %copy.8.refs_2_.refs_4_.refs_8_, ...), custom_call_target="tpu_custom_call" | custom-call | flops 1073741824 | bytes 6291456 | tf_op jit(solution)/shard_map/inner_band/pallas_call | solution.py:320
  53.7 0.0 collective-permute-done.refs_1_
  53.7 1.5 %band.1 = (f32[128,128]{1,0:T(8,128)S(1)}, f32[1024,128]{1,0:T(8,128)S(1)}) custom-call(f32[2048,128]{1,0:T(8,128)S(1)} %get-tuple-element.31.refs_0_, f32[512,128]{1,0:T(8,128)S(1)} %collective-permute-done.refs_1_, f32[512,128]{1,0:T(8,128)S(1)} %collective-permute-done.1.refs_2_, f32[1024,128]{1,0:T(8,128)S(1)} %get-tuple-element.34.refs_3_, ...), custom_call_target="tpu_custom_call" | custom-call | flops 1073741824 | bytes 6291456 | tf_op jit(solution)/shard_map/band/pallas_call | solution.py:331
  55.2 1.4 %collective-permute-start.6 = (f32[128,128]{1,0:T(8,128)S(1)}, f32[128,128]{1,0:T(8,128)S(1)}, u32[]{:S(2)}, u32[]{:S(2)}) collective-permute-start(f32[128,128]{1,0:T(8,128)S(1)} %get-tuple-element.50.refs_0_), channel_id=1, source_target_pairs={{0,1},{1,2},{2,3},{3,0},{4,5},{5,6},{6,7},{7,4},{8,9},{9,10},{10,1... | collective-permute-start | bytes 196616 | tf_op jit(solution)/shard_map/ppermute | solution.py:252
  56.6 2.6 %collective-permute-start.5 = (f32[128,128]{1,0:T(8,128)S(1)}, f32[128,128]{1,0:T(8,128)S(1)}, u32[]{:S(2)}, u32[]{:S(2)}) collective-permute-start(f32[128,128]{1,0:T(8,128)S(1)} %get-tuple-element.50.refs_0_), channel_id=1, source_target_pairs={{0,2},{1,3},{2,0},{3,1},{4,6},{5,7},{6,4},{7,5},{8,10},{9,11},{10,... | collective-permute-start | bytes 196616 | tf_op jit(solution)/shard_map/ppermute | solution.py:252
  59.2 1.1 %collective-permute-start.4 = (f32[128,128]{1,0:T(8,128)S(1)}, f32[128,128]{1,0:T(8,128)S(1)}, u32[]{:S(2)}, u32[]{:S(2)}) collective-permute-start(f32[128,128]{1,0:T(8,128)S(1)} %get-tuple-element.50.refs_0_), channel_id=1, source_target_pairs={{0,3},{1,0},{2,1},{3,2},{4,7},{5,4},{6,5},{7,6},{8,11},{9,8},{10,9... | collective-permute-start | bytes 196616 | tf_op jit(solution)/shard_map/ppermute | solution.py:252
  60.3 1.4 %collective-permute-done.5.refs_2_ = f32[128,128]{1,0:T(8,128)S(1)} collective-permute-done((f32[128,128]{1,0:T(8,128)S(1)}, f32[128,128]{1,0:T(8,128)S(1)}, u32[]{:S(2)}, u32[]{:S(2)}) %collective-permute-start.5) | collective-permute-done | bytes 65568 | tf_op jit(solution)/shard_map/ppermute | solution.py:252
  61.7 1.4 %collective-permute-done.4.refs_1_ = f32[128,128]{1,0:T(8,128)S(1)} collective-permute-done((f32[128,128]{1,0:T(8,128)S(1)}, f32[128,128]{1,0:T(8,128)S(1)}, u32[]{:S(2)}, u32[]{:S(2)}) %collective-permute-start.4) | collective-permute-done | bytes 65568 | tf_op jit(solution)/shard_map/ppermute | solution.py:252
  63.1 2.5 %gradient.1 = f32[2048,128]{1,0:T(8,128)S(1)} custom-call(f32[128,128]{1,0:T(8,128)S(1)} %get-tuple-element.50.refs_0_, f32[128,128]{1,0:T(8,128)S(1)} %collective-permute-done.4.refs_1_, f32[128,128]{1,0:T(8,128)S(1)} %collective-permute-done.5.refs_2_, f32[128,128]{1,0:T(8,128)S(1)} %collective-permute-done.6.refs_3_, ...), custom_call_target="tpu_custom_call" | custom-call | flops 2147483648 | bytes 5242880 | tf_op jit(solution)/shard_map/gradient/pallas_call | solution.py:341
  65.6 35.1 %all_to_all.10 = f32[64,2,4,4,128]{4,3,2,1,0:T(4,128)S(1)} all-to-all(f32[64,2,4,4,128]{4,3,2,1,0:T(4,128)S(1)} %bitcast.10), channel_id=1, replica_groups={{0,4,8,12,16,20,24,28,60,56,52,48,44,40,36,32,64,68,72,76,80,84,88,92,1..., dimensions={0} | all-to-all | bytes 2097152 | tf_op jit(solution)/shard_map/all_to_all | solution.py:257
  100.8 1.0 copy.11
  (12 shorter events, 0.1 us)
Async XLA Ops:
  0.0 13.2 %copy-start.3 = (s32[8192]{0:T(1024)S(1)}, s32[8192]{0:T(1024)}, u32[]{:S(2)}) copy-start(s32[8192]{0:T(1024)} %param.4) | copy-start | bytes 98308
  0.0 14.0 %copy-start = (f32[1024,4,128]{2,1,0:T(4,128)S(1)}, f32[1024,4,128]{2,1,0:T(4,128)}, u32[]{:S(2)}) copy-start(f32[1024,4,128]{2,1,0:T(4,128)} %potential.1) | copy-start | bytes 6291460
  0.0 41.4 %all-to-all-start = ((f32[64,32,128]{2,1,0:T(8,128)}), f32[64,32,128]{2,1,0:T(8,128)S(1)}, u32[]{:S(2)}, u32[]{:S(2)}) async-start(f32[64,32,128]{2,1,0:T(8,128)} %bitcast.12), calls=%async_computation | async-start | bytes 2097152 | tf_op jit(solution)/shard_map/all_to_all | solution.py:257
  15.6 1.0 copy-start.1
  42.4 8.0 %collective-permute-start.2 = (f32[768,128]{1,0:T(8,128)S(1)}, f32[768,128]{1,0:T(8,128)S(1)}, u32[]{:S(2)}, u32[]{:S(2)}) collective-permute-start(f32[768,128]{1,0:T(8,128)S(1)} %get-tuple-element.37), channel_id=1, source_target_pairs={{0,4},{4,8},{8,12},{12,16},{16,20},{20,24},{24,28},{28,60},{60,56}... | collective-permute-start | bytes 1179656 | tf_op jit(solution)/shard_map/ppermute | solution.py:252
  44.6 7.5 %collective-permute-start.3 = (f32[768,128]{1,0:T(8,128)S(1)}, f32[768,128]{1,0:T(8,128)S(1)}, u32[]{:S(2)}, u32[]{:S(2)}) collective-permute-start(f32[768,128]{1,0:T(8,128)S(1)} %get-tuple-element.38), channel_id=1, source_target_pairs={{0,224},{4,0},{8,4},{12,8},{16,12},{20,16},{24,20},{28,24},{60,28}... | collective-permute-start | bytes 1179656 | tf_op jit(solution)/shard_map/ppermute | solution.py:252
  44.6 9.0 %collective-permute-start = (f32[512,128]{1,0:T(8,128)}, f32[512,128]{1,0:T(8,128)S(1)}, u32[]{:S(2)}, u32[]{:S(2)}) collective-permute-start(f32[512,128]{1,0:T(8,128)} %get-tuple-element.32), channel_id=1, source_target_pairs={{0,1},{1,2},{2,3},{3,0},{4,5},{5,6},{6,7},{7,4},{8,9},{9,10},{10,1... | collective-permute-start | bytes 786440 | tf_op jit(solution)/shard_map/ppermute | solution.py:252
  45.9 7.8 %collective-permute-start.1 = (f32[512,128]{1,0:T(8,128)S(1)}, f32[512,128]{1,0:T(8,128)S(1)}, u32[]{:S(2)}, u32[]{:S(2)}) collective-permute-start(f32[512,128]{1,0:T(8,128)S(1)} %get-tuple-element.33), channel_id=1, source_target_pairs={{0,3},{1,0},{2,1},{3,2},{4,7},{5,4},{6,5},{7,6},{8,11},{9,8},{10,9... | collective-permute-start | bytes 786440 | tf_op jit(solution)/shard_map/ppermute | solution.py:252
  47.5 1.2 %copy-start.2 = (f32[2048,128]{1,0:T(8,128)S(1)}, f32[2048,128]{1,0:T(8,128)}, u32[]{:S(2)}) copy-start(f32[2048,128]{1,0:T(8,128)} %copy-done.1) | copy-start | bytes 3145732
  55.2 5.1 %collective-permute-start.6 = (f32[128,128]{1,0:T(8,128)S(1)}, f32[128,128]{1,0:T(8,128)S(1)}, u32[]{:S(2)}, u32[]{:S(2)}) collective-permute-start(f32[128,128]{1,0:T(8,128)S(1)} %get-tuple-element.50.refs_0_), channel_id=1, source_target_pairs={{0,1},{1,2},{2,3},{3,0},{4,5},{5,6},{6,7},{7,4},{8,9},{9,10},{10,1... | collective-permute-start | bytes 196616 | tf_op jit(solution)/shard_map/ppermute | solution.py:252
  56.6 5.1 %collective-permute-start.5 = (f32[128,128]{1,0:T(8,128)S(1)}, f32[128,128]{1,0:T(8,128)S(1)}, u32[]{:S(2)}, u32[]{:S(2)}) collective-permute-start(f32[128,128]{1,0:T(8,128)S(1)} %get-tuple-element.50.refs_0_), channel_id=1, source_target_pairs={{0,2},{1,3},{2,0},{3,1},{4,6},{5,7},{6,4},{7,5},{8,10},{9,11},{10,... | collective-permute-start | bytes 196616 | tf_op jit(solution)/shard_map/ppermute | solution.py:252
  59.2 3.9 %collective-permute-start.4 = (f32[128,128]{1,0:T(8,128)S(1)}, f32[128,128]{1,0:T(8,128)S(1)}, u32[]{:S(2)}, u32[]{:S(2)}) collective-permute-start(f32[128,128]{1,0:T(8,128)S(1)} %get-tuple-element.50.refs_0_), channel_id=1, source_target_pairs={{0,3},{1,0},{2,1},{3,2},{4,7},{5,4},{6,5},{7,6},{8,11},{9,8},{10,9... | collective-permute-start | bytes 196616 | tf_op jit(solution)/shard_map/ppermute | solution.py:252
